TPU v7x, 32 devices: a whole 2x2x4 slice. The times are simulated.
32 devices in a mesh: dp: 32 (over z, y, x, core).
Axes of the slice: x: 2, y: 2, z: 4, core: 2. Of those that a mesh axis runs over, the one named last changes fastest.
Arguments:
- tokens: bfloat16 [12288, 2048], P('dp'), may hold values from -6 to 6
- segments: int32 [32, 384], P('dp'), may hold values from 0 to 2, never falling along the last dimension, each value on 1 to 192 neighbouring positions
- w_query: bfloat16 [2048, 2048], P('dp'), may hold values from -0.125 to 0.125
- w_key: bfloat16 [2048, 1024], P('dp'), may hold values from -0.125 to 0.125
- w_value: bfloat16 [2048, 1024], P('dp'), may hold values from -0.125 to 0.125
- w_out: bfloat16 [2048, 2048], P('dp'), may hold values from -0.75 to 0.75
- w_gate: bfloat16 [2048, 6144], P('dp'), may hold values from -0.125 to 0.125
- w_up: bfloat16 [2048, 6144], P('dp'), may hold values from -0.125 to 0.125
- w_down: bfloat16 [6144, 2048], P('dp'), may hold values from -0.078125 to 0.078125
- attn_gain: bfloat16 [2048], P('dp'), may hold values from 0.5 to 1.5
- mlp_gain: bfloat16 [2048], P('dp'), may hold values from 0.5 to 1.5
- query_gain: bfloat16 [128], P('dp'), may hold values from 0.25 to 1.75
- key_gain: bfloat16 [128], P('dp'), may hold values from 0.25 to 1.75
- cotangent: bfloat16 [12288, 2048], P('dp'), may hold values from -6 to 6
Outputs:
- output: bfloat16 [12288, 2048], P('dp')
- tokens_grad: bfloat16 [12288, 2048], P('dp')
- w_query_grad: float32 [2048, 2048], P('dp')
- w_key_grad: float32 [2048, 1024], P('dp')
- w_value_grad: float32 [2048, 1024], P('dp')
- w_out_grad: float32 [2048, 2048], P('dp')
- w_gate_grad: float32 [2048, 6144], P('dp')
- w_up_grad: float32 [2048, 6144], P('dp')
- w_down_grad: float32 [6144, 2048], P('dp')
- attn_gain_grad: float32 [2048], P('dp')
- mlp_gain_grad: float32 [2048], P('dp')
- query_gain_grad: float32 [128], P('dp')
- key_gain_grad: float32 [128], P('dp')
Inputs may be any that keep to these rules, and one draw needn't show every extreme that they name: `segments`: document numbers never fall along a sequence and start at 0; each document spans 1 to 192 positions, and one spans exactly that many.
All inputs are finite; a program needn't handle non-finite values.
Results may differ from a plain program's by a relative error of at most 0.017.
Values may be sent and summed in bfloat16 or wider, within the bound.
A program may use at most 448 MiB of HBM per device.

v0:
```python
import functools

import jax
import jax.numpy as jnp
from jax import lax
from jax.experimental import pallas as pl
from jax.experimental.pallas import tpu as pltpu
from jax.sharding import PartitionSpec as P

H = 16
KVH = 8
HD = 128
TP = 4

EPS = 1e-06
THETA = 1000000.0

f32 = jnp.float32
bf16 = jnp.bfloat16
MESH = pl.DeviceIdType.MESH


def inverse_rms(values):
    return lax.rsqrt(jnp.mean(values * values, axis=-1, keepdims=True) + EPS)


def dot(a, b):
    return lax.dot_general(a, b, (((1,), (0,)), ((), ())), preferred_element_type=f32)


def dot_tn(a, b):
    return lax.dot_general(a, b, (((0,), (0,)), ((), ())), preferred_element_type=f32)


def dot_nt(a, b):
    return lax.dot_general(a, b, (((1,), (1,)), ((), ())), preferred_element_type=f32)


def turn(v):
    return pltpu.roll(v, HD // 2, 1)


def heads_of(raw, cosine, sine, query_gain, key_gain):
    out = []
    for k, gain in ((0, query_gain), (1, query_gain), (2, key_gain)):
        v = raw[:, k * HD : (k + 1) * HD]
        inverse = inverse_rms(v)
        normed = v * inverse * gain
        out.append((v, inverse, (normed * cosine + turn(normed) * sine).astype(bf16)))
    return out, raw[:, 3 * HD :].astype(bf16)


def block_probs(qs, keys, starts, row0, score_scale):
    size, span = starts.shape[0], keys.shape[0]
    scores = dot_nt(qs, keys) * score_scale
    column = lax.broadcasted_iota(jnp.int32, (size, span), 1)
    row = lax.broadcasted_iota(jnp.int32, (size, span), 0) + row0
    allowed = (column >= starts) & (column <= row)
    allowed = jnp.concatenate([allowed, allowed], axis=0)
    scores = jnp.where(allowed, scores, -1e30)
    power_term = jnp.exp(scores - jnp.max(scores, axis=-1, keepdims=True))
    return power_term / jnp.sum(power_term, axis=-1, keepdims=True)


def partners(me):
    x = me + 2 - 4 * ((me // 2) % 2)
    y = me + 4 - 8 * ((me // 4) % 2)
    d = x + 4 - 8 * ((me // 4) % 2)
    return x, y, d, me + 1 - 2 * (me % 2)


def greet(devices):
    barrier = pltpu.get_barrier_semaphore()
    for device in devices:
        pl.semaphore_signal(barrier, inc=1, device_id=(device,), device_id_type=MESH)
    pl.semaphore_wait(barrier, len(devices))


def remote(src, dst, send, recv, device):
    return pltpu.make_async_remote_copy(
        src_ref=src, dst_ref=dst, send_sem=send, recv_sem=recv, device_id=(device,), device_id_type=MESH
    )


TILE = 512


class Scatter:
    def __init__(self, out, ebuf, rd, rxy, send, recv, x, y):
        self.out, self.ebuf, self.rd, self.rxy = out, ebuf, rd, rxy
        length, width = out.shape
        h = length // 2
        self.half = h
        self.span = width // 2

        def pair(i, src, dst, rows, device):
            copies = []
            for c in range(2):
                cols = pl.ds(c * self.span, self.span)
                copies.append(
                    remote(
                        src[0].at[src[1], pl.ds(src[2], rows), cols],
                        dst[0].at[dst[1], pl.ds(dst[2], rows), cols],
                        send.at[i, c],
                        recv.at[i, c],
                        device,
                    )
                )
            return copies

        self.low = pair(0, (ebuf, 0, 0), (rd, 0, 0), h, y)
        self.high = pair(1, (ebuf, 0, h), (rd, 1, 0), h, x)
        self.to_x = pair(2, (ebuf, 1, 0), (rxy, 0, 0), length, x)
        self.to_y = pair(3, (ebuf, 2, 0), (rxy, 1, 0), length, y)

    def add(self, k, tile_of):
        h = self.half
        tiles = self.span // TILE
        for c in range(2):
            if k == 1:
                self.low[c].wait_recv()
            if k == 2:
                self.high[c].wait_recv()

            @pl.loop(c * tiles, (c + 1) * tiles)
            def _(t):
                sl = pl.ds(pl.multiple_of(t * TILE, TILE), TILE)
                value = tile_of(sl)
                if k == 0:
                    self.out[:, sl] = value
                elif k == 3:
                    self.ebuf[0, :, sl] = value.astype(bf16)
                elif k == 1:
                    self.ebuf[1, :h, sl] = (value[:h] + self.rd[0, :, sl].astype(f32)).astype(bf16)
                    self.ebuf[1, h:, sl] = value[h:].astype(bf16)
                else:
                    self.ebuf[2, :h, sl] = value[:h].astype(bf16)
                    self.ebuf[2, h:, sl] = (value[h:] + self.rd[1, :, sl].astype(f32)).astype(bf16)

            if k == 3:
                self.low[c].start()
                self.high[c].start()
            if k == 1:
                self.to_x[c].start()
            if k == 2:
                self.to_y[c].start()

    def finish(self):
        tiles = self.span // TILE
        for c in range(2):
            self.to_x[c].wait_recv()
            self.to_y[c].wait_recv()

            @pl.loop(c * tiles, (c + 1) * tiles)
            def _(t):
                sl = pl.ds(pl.multiple_of(t * TILE, TILE), TILE)
                self.out[:, sl] += self.rxy[0, :, sl].astype(f32) + self.rxy[1, :, sl].astype(f32)

        for copy in self.low + self.high + self.to_x + self.to_y:
            copy.wait_send()


def scatter_scratch(length, width):
    return [
        pltpu.VMEM((3, length, width), bf16),
        pltpu.VMEM((2, length // 2, width), bf16),
        pltpu.VMEM((2, length, width), bf16),
        pltpu.SemaphoreType.DMA((4, 2)),
        pltpu.SemaphoreType.DMA((4, 2)),
    ]


def attend_back_kernel(
    gm_ref, raw_ref, a1_ref, pa_ref, pb_ref, cos_ref, sin_ref, start_ref, qg_ref, kg_ref, mix_ref, dy_ref,
    out_ref, sum_ref, dqg_ref, dkg_ref, ogot_ref, orecv_ref,
    gp_ref, dk_ref, dv_ref, acc_a, acc_b, heads, cbuf, crecv, oslot, ofetch,
    ebuf, rd, rxy, rs_send, rs_recv, do_send, do_recv, do_own, c_send, c_recv,
    oc_send, oc_recv, os_send, os_recv, o_local,
):
    length = a1_ref.shape[0]
    step = 128
    score_scale = HD ** (-0.5)
    s = pl.program_id(0)
    me = lax.axis_index("dp")
    core = me % 2
    place = (me // 2) % TP
    x, y, d, sibling = partners(me)
    cols = 4 * HD

    def columns_of(device):
        return pl.ds(pl.multiple_of(((device // 2) % TP) * cols, cols), cols)

    incoming = [
        remote(gm_ref.at[:, columns_of(device)], heads.at[k], do_send.at[k - 1], do_recv.at[k - 1], device)
        for k, device in ((1, x), (2, y), (3, d))
    ]
    own = pltpu.make_async_copy(
        gm_ref.at[:, pl.ds(pl.multiple_of(place * cols, cols), cols)], heads.at[0], do_own
    )
    scatter = Scatter(out_ref, ebuf, rd, rxy, rs_send, rs_recv, x, y)
    across = remote(cbuf, crecv, c_send, c_recv, sibling)
    block = oslot.shape[2]
    o_across = [
        remote(oslot.at[k], orecv_ref.at[k], oc_send.at[k], oc_recv.at[k], sibling) for k in range(TP)
    ]
    tall = oslot.shape[1] // 2
    o_low = remote(
        oslot.at[3, pl.ds(0, tall)], ogot_ref.at[2, pl.ds(0, tall)], os_send.at[2], os_recv.at[2], y
    )
    o_high = remote(
        oslot.at[3, pl.ds(tall, tall)], ogot_ref.at[2, pl.ds(tall, tall)], os_send.at[3], os_recv.at[3], x
    )
    o_home = [
        remote(oslot.at[k], ogot_ref.at[k - 1], os_send.at[k - 1], os_recv.at[k - 1], device)
        for k, device in ((1, x), (2, y))
    ]
    o_back = [
        pltpu.make_async_copy(ogot_ref.at[k - 1], oslot.at[k], o_local.at[k]) for k in range(1, 3)
    ]

    def out_block(k, side):
        device = (me, x, y, d)[k]
        at = ((device // 2) % TP) * 2 + side
        return pl.ds(pl.multiple_of(at * block, block), block)

    def out_tile(k, side, sl):
        return dot_tn(mix_ref[:, sl], dy_ref[:, out_block(k, side)])

    @pl.when(s == 0)
    def _():
        greet((x, y, d, sibling))
        for k in (2, 0, 1):
            incoming[k].start()
        own.start()
        for ref in (acc_a, acc_b, dqg_ref, dkg_ref):
            ref[...] = jnp.zeros_like(ref)
        for k in (3, 1, 2, 0):

            @pl.loop(0, oslot.shape[1] // TILE)
            def _(t):
                sl = pl.ds(pl.multiple_of(t * TILE, TILE), TILE)
                oslot[k, sl, :] = out_tile(k, 1 - core, sl).astype(bf16)

            o_across[k].start()
        incoming[2].wait_recv()

    @pl.when(s == 1)
    def _():
        for k in (3, 1, 2, 0):
            o_across[k].wait_send()
            o_across[k].wait_recv()
            fetch = pltpu.make_async_copy(orecv_ref.at[k], ofetch, o_local.at[0])
            fetch.start()
            fetch.wait()

            @pl.loop(0, oslot.shape[1] // TILE)
            def _(t):
                sl = pl.ds(pl.multiple_of(t * TILE, TILE), TILE)
                oslot[k, sl, :] = (out_tile(k, core, sl) + ofetch[sl, :].astype(f32)).astype(bf16)

            if k == 3:
                o_low.start()
                o_high.start()
        incoming[0].wait_recv()

    @pl.when(s == 2)
    def _():
        for copy, k, offset in ((o_low, 1, 0), (o_high, 2, tall)):
            copy.wait_recv()
            fetch = pltpu.make_async_copy(
                ogot_ref.at[2, pl.ds(offset, tall)], ofetch.at[pl.ds(0, tall)], o_local.at[0]
            )
            fetch.start()
            fetch.wait()

            @pl.loop(0, tall // TILE)
            def _(t):
                sl = pl.ds(pl.multiple_of(t * TILE, TILE), TILE)
                to = pl.ds(pl.multiple_of(offset + t * TILE, TILE), TILE)
                oslot[k, to, :] = (oslot[k, to, :].astype(f32) + ofetch[sl, :].astype(f32)).astype(bf16)

            o_home[k - 1].start()
        incoming[1].wait_recv()

    @pl.when(s == 3)
    def _():
        own.wait()

    which = part_order(s)

    for h in range(2):
        col = h * 4 * HD
        side = core if h == 0 else 1 - core
        cosine, sine = cos_ref[...], sin_ref[...]
        (q0, q1, k0), value = heads_of(
            raw_ref[:, col : col + 4 * HD], cosine, sine, qg_ref[...], kg_ref[...]
        )
        dk_ref[...] = jnp.zeros_like(dk_ref)
        dv_ref[...] = jnp.zeros_like(dv_ref)
        parts = []
        for b in range(length // step):
            sl = slice(b * step, (b + 1) * step)
            span = (b + 1) * step
            qs = jnp.concatenate([q0[2][sl], q1[2][sl]], axis=0)
            gs = jnp.concatenate(
                [
                    heads[which, sl, pl.ds(pl.multiple_of((2 * side + g) * HD, HD), HD)]
                    for g in range(2)
                ],
                axis=0,
            )
            keys, values = k0[2][:span], value[:span]
            probs = block_probs(qs, keys, start_ref[sl, :], b * step, score_scale)
            dv_ref[:span, :] += dot_tn(probs.astype(bf16), gs)
            grad_probs = dot_nt(gs, values)
            delta = jnp.sum(probs * grad_probs, axis=-1, keepdims=True)
            grad_scores = (probs * (grad_probs - delta)).astype(bf16)
            dk_ref[:span, :] += dot_tn(grad_scores, qs)
            parts.append(dot(grad_scores, keys))
        dq0 = jnp.concatenate([p[:step] for p in parts], axis=0) * score_scale
        dq1 = jnp.concatenate([p[step:] for p in parts], axis=0) * score_scale
        for k, (raw, inverse, _), grad, gain_ref, dgain_ref in (
            (0, q0, dq0, qg_ref, dqg_ref),
            (1, q1, dq1, qg_ref, dqg_ref),
            (2, k0, dk_ref[...] * score_scale, kg_ref, dkg_ref),
        ):
            back = grad * cosine + turn(grad * sine)
            scaled = back * gain_ref[...]
            inner = jnp.mean(scaled * raw, axis=-1, keepdims=True)
            gp_ref[:, col + k * HD : col + (k + 1) * HD] = (
                inverse * (scaled - raw * inverse * inverse * inner)
            ).astype(bf16)
            dgain_ref[...] += jnp.sum(back * raw * inverse, axis=0, keepdims=True)
        gp_ref[:, col + 3 * HD : col + 4 * HD] = dv_ref[...].astype(bf16)

    half = 4 * HD

    def tile_of(sl):
        return dot_nt(gp_ref[:, :half], pa_ref[sl, :]) + dot_nt(gp_ref[:, half:], pb_ref[sl, :])

    for at, k in enumerate(ORDER):

        @pl.when(s == at)
        def _():
            scatter.add(k, tile_of)

    @pl.loop(0, acc_a.shape[0] // TILE)
    def _(t):
        sl = pl.ds(pl.multiple_of(t * TILE, TILE), TILE)
        acc_b[sl, :] += dot_tn(a1_ref[:, sl], gp_ref[:, half:])

    @pl.when(s == 3)
    def _():
        cbuf[...] = acc_b[...].astype(bf16)
        across.start()

    @pl.loop(0, acc_a.shape[0] // TILE)
    def _(t):
        sl = pl.ds(pl.multiple_of(t * TILE, TILE), TILE)
        acc_a[sl, :] += dot_tn(a1_ref[:, sl], gp_ref[:, :half])

    @pl.when(s == 3)
    def _():
        proj = acc_a.shape[1]
        across.wait_recv()
        sum_ref[:, :proj] = (acc_a[...] + crecv[...].astype(f32)).astype(bf16)
        o_low.wait_send()
        o_high.wait_send()
        for copy, back in zip(o_home, o_back):
            copy.wait()
            back.start()
        for back in o_back:
            back.wait()

        @pl.loop(0, oslot.shape[1] // TILE)
        def _(t):
            sl = pl.ds(pl.multiple_of(t * TILE, TILE), TILE)
            total = oslot[0, sl, :].astype(f32)
            for k in range(1, 3):
                total += oslot[k, sl, :].astype(f32)
            sum_ref[sl, proj:] = total.astype(bf16)

        scatter.finish()
        across.wait_send()
        for copy in incoming:
            copy.wait_send()


CHUNK = 256


def feed_kernel(
    a2_ref, wa_ref, g_ref,
    gate_ref, up_ref, hid_ref, wb_ref, ga_ref, sum_ref,
    a2, wa, wb, g, hid, stage, cbuf, crecv, acc,
    loads, x_send, x_recv, g_send, g_recv, s_sem, c_send, c_recv, keeps,
):
    tokens, width = a2.shape
    length = g_ref.shape[0]
    fn = wa.shape[1] // 2
    x, y, d, sibling = partners(lax.axis_index("dp"))
    h = length // 2

    def rows(k, offset=0, size=length):
        return g.at[pl.ds(k * length + offset, size)]

    load_x = pltpu.make_async_copy(a2_ref, a2, loads.at[0])
    load_w = pltpu.make_async_copy(wa_ref, wa, loads.at[1])
    load_g = pltpu.make_async_copy(g_ref, rows(0), loads.at[2])
    swap_w = remote(wa_ref, wb, x_send.at[0], x_recv.at[0], sibling)
    g_x = remote(g_ref, rows(1), g_send.at[0], g_recv.at[0], x)
    g_y = remote(g_ref, rows(2), g_send.at[1], g_recv.at[1], y)
    g_low = remote(rows(2, 0, h), rows(3, 0, h), g_send.at[2], g_recv.at[2], x)
    g_high = remote(rows(1, h, h), rows(3, h, h), g_send.at[3], g_recv.at[3], y)
    keep_w = pltpu.make_async_copy(wb, wb_ref, keeps.at[0])
    keep_g = pltpu.make_async_copy(g, ga_ref, keeps.at[1])
    keep_h = pltpu.make_async_copy(hid, hid_ref, keeps.at[2])

    load_w.start()
    load_x.start()
    load_g.start()
    greet((x, y, d, sibling))
    g_x.start()
    g_y.start()
    swap_w.start()

    per_half = fn // CHUNK
    span = 2 * length
    halves = tokens // span

    def store(i, which, ref):
        half = i // (per_half * halves)
        j = i % (per_half * halves)
        r, c = j // per_half, j % per_half
        return pltpu.make_async_copy(
            stage.at[i % 2, which],
            ref.at[
                pl.ds(pl.multiple_of(r * span, span), span),
                pl.ds(pl.multiple_of((half * per_half + c) * CHUNK, CHUNK), CHUNK),
            ],
            s_sem.at[i % 2, which],
        )

    def run(half, w):
        @pl.loop(0, per_half * halves)
        def _(j):
            i = j + half * per_half * halves

            @pl.when(i >= 2)
            def _():
                store(i - 2, 0, gate_ref).wait()
                store(i - 2, 1, up_ref).wait()

            r, c = j // per_half, j % per_half
            sl = pl.ds(pl.multiple_of(r * span, span), span)
            gate = dot(a2[sl, :], w[:, pl.ds(pl.multiple_of(c * CHUNK, CHUNK), CHUNK)])
            up = dot(a2[sl, :], w[:, pl.ds(pl.multiple_of(fn + c * CHUNK, CHUNK), CHUNK)])
            stage[i % 2, 0] = gate.astype(bf16)
            stage[i % 2, 1] = up.astype(bf16)
            hid[sl, pl.ds(pl.multiple_of((half * per_half + c) * CHUNK, CHUNK), CHUNK)] = (
                gate * jax.nn.sigmoid(gate) * up
            ).astype(bf16)
            store(i, 0, gate_ref).start()
            store(i, 1, up_ref).start()

    load_w.wait()
    load_x.wait()
    run(0, wa)
    swap_w.wait_recv()
    keep_w.start()
    run(1, wb)
    last = 2 * per_half * halves
    for i in (last - 2, last - 1):
        store(i, 0, gate_ref).wait()
        store(i, 1, up_ref).wait()
    keep_h.start()

    g_x.wait_recv()
    g_high.start()
    g_y.wait_recv()
    g_low.start()
    load_g.wait()
    near = pl.ds(0, 3 * length)
    far = pl.ds(3 * length, length)

    @pl.loop(0, 2 * per_half)
    def _(t):
        cols = pl.ds(pl.multiple_of(t * CHUNK, CHUNK), CHUNK)
        acc[t] = dot_tn(hid[near, cols], g[near, :])

    g_low.wait_recv()
    g_high.wait_recv()
    keep_g.start()

    def across(t):
        return remote(cbuf.at[t], crecv.at[t], c_send.at[t], c_recv.at[t], sibling)

    @pl.loop(0, per_half)
    def _(t):
        cols = pl.ds(pl.multiple_of(fn + t * CHUNK, CHUNK), CHUNK)
        cbuf[t] = (acc[per_half + t] + dot_tn(hid[far, cols], g[far, :])).astype(bf16)
        across(t).start()

    @pl.loop(0, per_half)
    def _(t):
        cols = pl.ds(pl.multiple_of(t * CHUNK, CHUNK), CHUNK)
        own = acc[t] + dot_tn(hid[far, cols], g[far, :])
        across(t).wait_recv()
        sum_ref[cols, :] = (own + crecv[t].astype(f32)).astype(bf16)

    for t in range(per_half):
        across(t).wait_send()
    for copy in (swap_w, g_x, g_y, g_low, g_high):
        copy.wait_send()
    for copy in (keep_w, keep_g, keep_h):
        copy.wait()


def feed_forward(a2, wa, g):
    tokens, width = a2.shape
    fn = wa.shape[1] // 2
    length = g.shape[0]
    anywhere = pl.BlockSpec(memory_space=pl.ANY)
    sem = pltpu.SemaphoreType.DMA
    return pl.pallas_call(
        feed_kernel,
        in_specs=[anywhere] * 3,
        out_specs=[anywhere] * 5 + [pl.BlockSpec(memory_space=pltpu.VMEM)],
        out_shape=[
            struct((tokens, 2 * fn), bf16),
            struct((tokens, 2 * fn), bf16),
            struct((tokens, 2 * fn), bf16),
            struct(wa.shape, bf16),
            struct((tokens, width), bf16),
            struct((fn, width), bf16),
        ],
        scratch_shapes=[
            pltpu.VMEM(a2.shape, bf16),
            pltpu.VMEM(wa.shape, bf16),
            pltpu.VMEM(wa.shape, bf16),
            pltpu.VMEM(a2.shape, bf16),
            pltpu.VMEM((tokens, 2 * fn), bf16),
            pltpu.VMEM((2, 2, 2 * length, CHUNK), bf16),
            pltpu.VMEM((fn // CHUNK, CHUNK, width), bf16),
            pltpu.VMEM((fn // CHUNK, CHUNK, width), bf16),
            pltpu.VMEM((2 * fn // CHUNK, CHUNK, width), f32),
            sem((3,)), sem((2,)), sem((2,)), sem((4,)), sem((4,)), sem((2, 2)),
            sem((fn // CHUNK,)), sem((fn // CHUNK,)), sem((3,)),
        ],
        compiler_params=pltpu.CompilerParams(
            vmem_limit_bytes=58 << 20, collective_id=4, has_side_effects=True
        ),
        cost_estimate=pl.CostEstimate(
            flops=4 * tokens * width * fn, bytes_accessed=30 << 20, transcendentals=0
        ),
        name="feed_forward",
    )(a2, wa, g)


def feed_back_kernel(
    gate_ref, up_ref, ga_ref, da_ref, wa_ref, wb_ref, a2_ref,
    out_ref, sum_ref, db_ref, crecv_ref,
    gp, wa, wb, a2, wd, uv, cbuf, cgot, stage, loads, u_sem, c_send, c_recv, g_sem, s_sem,
    d_send, d_recv,
    ebuf, rd, rxy, rs_send, rs_recv,
):
    length = out_ref.shape[0]
    cols = wa.shape[1]
    fn = cols // 2
    rows = cbuf.shape[1]
    tiles = a2.shape[1] // rows
    x, y, d, sibling = partners(lax.axis_index("dp"))
    scatter = Scatter(out_ref, ebuf, rd, rxy, rs_send, rs_recv, x, y)

    def piece(k):
        sl = pl.ds(k * length, length)
        return pltpu.make_async_copy(ga_ref.at[sl], a2.at[sl], loads.at[k])

    load_a = pltpu.make_async_copy(wa_ref, wa, loads.at[4])
    load_b = pltpu.make_async_copy(wb_ref, wb, loads.at[5])
    load_da = pltpu.make_async_copy(da_ref, wd.at[pl.ds(0, fn)], loads.at[6])
    swap_d = remote(da_ref, wd.at[pl.ds(fn, fn)], d_send, d_recv, sibling)
    keep_d = pltpu.make_async_copy(wd.at[pl.ds(fn, fn)], db_ref, loads.at[7])
    load_x = pltpu.make_async_copy(a2_ref, a2, loads.at[8])
    steps = 2 * TP

    def step_of(i):
        return part_order(i // 2), i % 2

    def fetch_uv(i, which, ref):
        part, c = step_of(i)
        return pltpu.make_async_copy(
            ref.at[
                pl.ds(pl.multiple_of(part * length, length), length),
                pl.ds(pl.multiple_of(c * fn, CHUNK), fn),
            ],
            uv.at[i % 2, which],
            u_sem.at[i % 2, which],
        )

    fetch_uv(0, 0, gate_ref).start()
    fetch_uv(0, 1, up_ref).start()
    piece(3).start()
    load_da.start()
    greet((x, y, d, sibling))
    swap_d.start()
    load_a.start()
    load_b.start()
    for k in (1, 2, 0):
        piece(k).start()

    def rows_of(t):
        return pl.ds(pl.multiple_of(t * rows, rows), rows)

    def across(t):
        return remote(
            cbuf.at[t % 2], crecv_ref.at[rows_of(t)], c_send.at[t % 2], c_recv.at[t], sibling
        )

    def fetch(t):
        return pltpu.make_async_copy(crecv_ref.at[rows_of(t)], cgot.at[t % 2], g_sem.at[t % 2])

    def store(t):
        return pltpu.make_async_copy(stage.at[t % 2], sum_ref.at[rows_of(t)], s_sem.at[t % 2])

    def part_of(k):
        sl = slice(k * length, (k + 1) * length)

        def tile_of(cut):
            return dot_nt(gp[sl, :cols], wa[cut, :]) + dot_nt(gp[sl, cols:], wb[cut, :])

        return tile_of

    def inner(first, end):
        @pl.loop(first, end)
        def _(i):
            @pl.when(i + 1 < steps)
            def _():
                fetch_uv(i + 1, 0, gate_ref).start()
                fetch_uv(i + 1, 1, up_ref).start()

            part, half = step_of(i)
            sl = pl.ds(pl.multiple_of(part * length, length), length)
            fetch_uv(i, 0, gate_ref).wait()
            fetch_uv(i, 1, up_ref).wait()
            for at in range(0, fn, CHUNK):
                cut = slice(at, at + CHUNK)
                rows_at = pl.ds(pl.multiple_of(half * fn + at, CHUNK), CHUNK)
                grad_hidden = dot_nt(a2[sl, :], wd[rows_at, :])
                gate = uv[i % 2, 0, :, cut].astype(f32)
                up = uv[i % 2, 1, :, cut].astype(f32)
                sig = jax.nn.sigmoid(gate)
                scaled = grad_hidden * sig
                to = half * cols + at
                gp[sl, pl.ds(pl.multiple_of(to, CHUNK), CHUNK)] = (
                    scaled * up * (1.0 + gate * (1.0 - sig))
                ).astype(bf16)
                gp[sl, pl.ds(pl.multiple_of(to + fn, CHUNK), CHUNK)] = (scaled * gate).astype(bf16)

    piece(3).wait()
    load_da.wait()
    inner(0, 1)
    swap_d.wait_recv()
    keep_d.start()
    inner(1, 2)
    load_a.wait()
    load_b.wait()
    scatter.add(3, part_of(3))
    for k in (1, 2, 0):
        piece(k).wait()
    inner(2, steps)
    load_x.start()
    scatter.add(1, part_of(1))
    scatter.add(2, part_of(2))
    load_x.wait()

    @pl.loop(0, tiles)
    def _(t):
        @pl.when(t >= 2)
        def _():
            across(t - 2).wait_send()

        cbuf[t % 2] = dot_tn(a2[:, rows_of(t)], gp[:, cols:]).astype(bf16)
        across(t).start()

    scatter.add(0, part_of(0))

    @pl.loop(0, tiles)
    def _(t):
        across(t).wait_recv()
        fetch(t).start()

        @pl.when(t >= 2)
        def _():
            store(t - 2).wait()

        own = dot_tn(a2[:, rows_of(t)], gp[:, :cols])
        fetch(t).wait()
        stage[t % 2] = (own + cgot[t % 2].astype(f32)).astype(bf16)
        store(t).start()

    for t in (tiles - 2, tiles - 1):
        store(t).wait()
        across(t).wait_send()
    swap_d.wait_send()
    keep_d.wait()
    scatter.finish()


def feed_backward(gate, up, ga, da, wa, wb, a2, length):
    tokens, width = a2.shape
    cols = wa.shape[1]
    rows = 256
    anywhere = pl.BlockSpec(memory_space=pl.ANY)
    sem = pltpu.SemaphoreType.DMA
    return pl.pallas_call(
        feed_back_kernel,
        in_specs=[anywhere] * 7,
        out_specs=[pl.BlockSpec(memory_space=pltpu.VMEM), anywhere, anywhere, anywhere],
        out_shape=[
            struct((length, width), f32),
            struct(wa.shape, bf16),
            struct(da.shape, bf16),
            struct(wa.shape, bf16),
        ],
        scratch_shapes=[
            pltpu.VMEM((tokens, 2 * cols), bf16),
            pltpu.VMEM(wa.shape, bf16),
            pltpu.VMEM(wb.shape, bf16),
            pltpu.VMEM(a2.shape, bf16),
            pltpu.VMEM((cols, width), bf16),
            pltpu.VMEM((2, 2, length, cols // 2), bf16),
            pltpu.VMEM((2, rows, cols), bf16),
            pltpu.VMEM((2, rows, cols), bf16),
            pltpu.VMEM((2, rows, cols), bf16),
            sem((9,)), sem((2, 2)), sem((2,)), sem((width // rows,)), sem((2,)), sem((2,)),
            sem, sem,
        ]
        + scatter_scratch(length, width),
        compiler_params=pltpu.CompilerParams(
            vmem_limit_bytes=62 << 20, collective_id=1, has_side_effects=True
        ),
        cost_estimate=pl.CostEstimate(
            flops=4 * tokens * width * cols, bytes_accessed=30 << 20, transcendentals=0
        ),
        name="feed_backward",
    )(gate, up, ga, da, wa, wb, a2)[:3]


ORDER = (3, 1, 2, 0)


def part_order(s):
    return 3 - 2 * s + 3 * (s // 2)


def rows_spec(length, cols):
    return pl.BlockSpec((length, cols), lambda s: (s, 0))


def whole_spec(shape):
    return pl.BlockSpec(shape, lambda s: (0, 0))


def struct(shape, dtype):
    return jax.ShapeDtypeStruct(shape, dtype)


def everyone(me):
    size = 2 * TP
    base = me - me % size
    return [base + (me % size + i) % size for i in range(1, size)]


def spread_kernel(
    wq_ref, wk_ref, wv_ref, wo_ref, gain_ref, seg_ref,
    all_ref, gains_ref, segs_ref,
    send, recv, local, s_send, s_recv,
):
    me = lax.axis_index("dp")
    size = 2 * TP
    rows = wq_ref.shape[0]
    here = pl.ds(pl.multiple_of((me % size) * rows, rows), rows)
    plan = []
    at = 0
    for ref in (wq_ref, wk_ref, wv_ref, wo_ref):
        width = ref.shape[1] // size
        plan.append((ref, width, all_ref.at[here, pl.ds(at, width)]))
        at += width

    def columns(ref, width, device):
        return ref.at[:, pl.ds(pl.multiple_of((device % size) * width, width), width)]

    others = everyone(me)
    gains_here = gains_ref.at[me % size]
    own = [
        pltpu.make_async_copy(columns(ref, width, me), dst, local.at[t])
        for t, (ref, width, dst) in enumerate(plan)
    ] + [
        pltpu.make_async_copy(gain_ref, gains_here, local.at[4]),
        pltpu.make_async_copy(seg_ref, segs_ref.at[0], local.at[5]),
    ]
    copies = [
        remote(columns(ref, width, device), dst, send.at[i, t], recv.at[i, t], device)
        for i, device in enumerate(others)
        for t, (ref, width, dst) in enumerate(plan)
    ]
    copies += [
        remote(gain_ref, gains_here, send.at[i, 4], recv.at[i, 4], device)
        for i, device in enumerate(others)
    ]
    copies += [
        remote(seg_ref, segs_ref.at[1 + k], s_send.at[k], s_recv.at[k], device)
        for k, device in enumerate(partners(me)[:3])
    ]
    for copy in own:
        copy.start()
    greet(others)
    for copy in copies:
        copy.start()
    for copy in own + copies:
        copy.wait()


def spread_attention(wq, wk, wv, wo, gain, seg):
    size = 2 * TP
    rows = wq.shape[0]
    cols = (wq.shape[1] + wk.shape[1] + wv.shape[1] + wo.shape[1]) // size
    anywhere = pl.BlockSpec(memory_space=pl.ANY)
    sem = pltpu.SemaphoreType.DMA
    return pl.pallas_call(
        spread_kernel,
        in_specs=[anywhere] * 6,
        out_specs=[anywhere] * 3,
        out_shape=[
            struct((size * rows, cols), bf16),
            struct((size, *gain.shape), f32),
            struct((TP, *seg.shape), jnp.int32),
        ],
        scratch_shapes=[sem((size - 1, 5)), sem((size - 1, 5)), sem((6,)), sem((3,)), sem((3,))],
        compiler_params=pltpu.CompilerParams(collective_id=5, has_side_effects=True),
        name="spread_attention",
    )(wq, wk, wv, wo, gain, seg)


def gather_kernel(
    run, seg_ref, rate_ref, x_ref, gate_ref, up_ref,
    cos_ref, sin_ref, start_ref, x_all, w_all,
    w_ref, flat, wide, xs, x_send, x_recv, w_send, w_recv, local,
):
    me = lax.axis_index("dp")
    size = 2 * TP
    x, y, d, _ = partners(me)
    others = everyone(me)
    length = x_ref.shape[0]
    rows = w_ref.shape[1]
    h = length // 2
    here = pl.ds(pl.multiple_of((me % size) * rows, rows), rows)

    def place(k, offset=0, count=length):
        return x_all.at[pl.ds(k * length + offset, count)]

    own = [
        pltpu.make_async_copy(xs, place(0), local.at[0]),
        pltpu.make_async_copy(w_ref.at[me % size], w_all.at[here], local.at[1]),
    ]
    fills = [
        pltpu.make_async_copy(ref, flat.at[i], local.at[2 + i]) for i, ref in enumerate((gate_ref, up_ref))
    ]
    weights = [
        remote(w_ref.at[device % size], w_all.at[here], w_send.at[i], w_recv.at[i], device)
        for i, device in enumerate(others)
    ]
    to_x = remote(xs, place(1), x_send.at[0], x_recv.at[0], x)
    to_y = remote(xs, place(2), x_send.at[1], x_recv.at[1], y)
    load_x = pltpu.make_async_copy(x_ref, xs, local.at[4])
    low = remote(place(2, 0, h), place(3, 0, h), x_send.at[2], x_recv.at[2], x)
    high = remote(place(1, h, h), place(3, h, h), x_send.at[3], x_recv.at[3], y)
    for copy in [load_x] + fills:
        copy.start()
    greet(others)
    load_x.wait()
    for copy in (to_x, to_y, own[0]):
        copy.start()
    for copy in fills:
        copy.wait()
    half = wide.shape[1] // 2
    values = [flat[i].astype(f32) for i in range(2)]
    for s in range(size):
        for i in range(2):
            for g in range(half // run):
                at = (g * size + s) * run
                wide[:, i * half + g * run : i * half + (g + 1) * run] = values[i][:, at : at + run]
        w_ref[s] = wide[...].astype(bf16)
    for copy in own[1:] + weights:
        copy.start()

    row = lax.broadcasted_iota(jnp.int32, (length, length), 0)
    column = lax.broadcasted_iota(jnp.int32, (length, length), 1)
    for k in range(TP):
        label = jnp.broadcast_to(seg_ref[k].astype(f32), (length, length))
        mine = jnp.sum(jnp.where(row == column, label, 0.0), axis=1, keepdims=True)
        start = jnp.sum(jnp.where(label < mine, 1.0, 0.0), axis=1, keepdims=True)
        position = lax.broadcasted_iota(jnp.int32, (length, 1), 0).astype(f32) - start
        angle = position * rate_ref[0:1, :]
        sl = pl.ds(k * length, length)
        cos_ref[sl, :] = jnp.cos(angle)
        sin_ref[sl, :] = jnp.sin(angle) * rate_ref[1:2, :]
        start_ref[sl, :] = start.astype(jnp.int32)

    to_x.wait_recv()
    high.start()
    to_y.wait_recv()
    low.start()
    for copy in (to_x, to_y):
        copy.wait_send()
    for copy in own + weights + [low, high]:
        copy.wait()


def gather_group(seg, rates, x, gate, up, run):
    size = 2 * TP
    rows, cols = gate.shape[0], 2 * gate.shape[1] // size
    anywhere = pl.BlockSpec(memory_space=pl.ANY)
    vmem = pl.BlockSpec(memory_space=pltpu.VMEM)
    sem = pltpu.SemaphoreType.DMA
    return pl.pallas_call(
        functools.partial(gather_kernel, run),
        in_specs=[vmem] * 2 + [anywhere] * 3,
        out_specs=[vmem] * 3 + [anywhere] * 2,
        out_shape=[
            struct((TP * x.shape[0], HD), f32),
            struct((TP * x.shape[0], HD), f32),
            struct((TP * x.shape[0], 1), jnp.int32),
            struct((TP * x.shape[0], x.shape[1]), bf16),
            struct((size * rows, cols), bf16),
        ],
        scratch_shapes=[
            pltpu.VMEM((size, rows, cols), bf16),
            pltpu.VMEM((2, *gate.shape), bf16),
            pltpu.VMEM((rows, cols), f32),
            pltpu.VMEM(x.shape, bf16),
            sem((4,)), sem((4,)), sem((size - 1,)), sem((size - 1,)), sem((5,)),
        ],
        compiler_params=pltpu.CompilerParams(
            vmem_limit_bytes=60 << 20, collective_id=6, has_side_effects=True
        ),
        name="gather_group",
    )(seg, rates, x, gate, up)


def attend_kernel(
    x_ref, cos_ref, sin_ref, start_ref, ag_ref, mg_ref, qg_ref, kg_ref, all_ref,
    raw_ref, a1_ref, mixed_ref, after_ref, inv_ref, pa_out, pb_out, wo_ref, a2_ref,
    pa_ref, pb_ref, fill, heads, mix, wo, a2, p_send, p_recv, o_send, o_recv, w_send, w_recv, s_send, s_recv, a_send, a_recv, local,
):
    length, width = x_ref.shape
    step = 128
    score_scale = HD ** (-0.5)
    s = pl.program_id(0)
    me = lax.axis_index("dp")
    core = me % 2
    place = (me // 2) % TP
    x, y, d, sibling = partners(me)
    near = (x, y, d)
    cols = 4 * HD
    proj = pa_ref.shape[1]
    block = all_ref.shape[2] - proj
    planes = all_ref.shape[0]
    deep = pa_ref.shape[0] // planes

    def block_of(device):
        return pl.ds(pl.multiple_of((device % (2 * TP)) * block, block), block)

    own_out = wo.at[:, block_of(me)]
    fills = []
    for g in range(planes):
        at = pl.ds(g * deep, deep)
        fills.append(
            pltpu.make_async_copy(
                all_ref.at[g, pl.ds(0, deep), pl.ds(0, proj)], pa_ref.at[at], fill.at[g, 0]
            )
        )
        fills.append(
            pltpu.make_async_copy(
                all_ref.at[g, pl.ds(0, deep), pl.ds(proj, block)], wo.at[at, block_of(me)], fill.at[g, 1]
            )
        )

    tall = wo.shape[0] // 2
    spread_out = [
        remote(own_out, own_out, w_send.at[i], w_recv.at[i], device)
        for i, device in enumerate(near[:2])
    ]

    def passed(device, offset, i, to):
        ref = wo.at[pl.ds(offset, tall), block_of(device)]
        return remote(ref, ref, w_send.at[i], w_recv.at[i], to)

    pass_on = [passed(x, tall, 2, y), passed(y, 0, 3, x)]
    beside = [remote(own_out, own_out, s_send.at[3], s_recv.at[3], sibling)]
    onward = [
        remote(wo.at[:, block_of(device)], wo.at[:, block_of(device)], s_send.at[i], s_recv.at[i], sibling)
        for i, device in enumerate(near)
    ]
    mine = pl.ds(pl.multiple_of(place * cols, cols), cols)
    home = [
        remote(heads.at[i + 1], mix.at[:, mine], o_send.at[i], o_recv.at[i], device)
        for i, device in enumerate(near)
    ]
    h = length // 2
    a2_x = remote(a2.at[0], a2.at[1], a_send.at[0], a_recv.at[0], x)
    a2_y = remote(a2.at[0], a2.at[2], a_send.at[1], a_recv.at[1], y)
    a2_low = remote(a2.at[2, pl.ds(0, h)], a2.at[3, pl.ds(0, h)], a_send.at[2], a_recv.at[2], x)
    a2_high = remote(a2.at[1, pl.ds(h, h)], a2.at[3, pl.ds(h, h)], a_send.at[3], a_recv.at[3], y)
    keep = [
        pltpu.make_async_copy(a2.at[k], a2_ref.at[pl.ds(k * length, length)], local.at[1 + k])
        for k in range(TP)
    ]
    keep_out = pltpu.make_async_copy(wo, wo_ref, local.at[5])
    keep_b = pltpu.make_async_copy(pb_ref, pb_out, local.at[6])
    keep_a = pltpu.make_async_copy(pa_ref, pa_out, local.at[0])
    swap_p = remote(pa_ref, pb_ref, p_send, p_recv, sibling)

    @pl.when(s == 0)
    def _():
        for copy in fills:
            copy.start()
        greet((x, y, d, sibling))
        for copy in fills:
            copy.wait()
        for copy in [swap_p] + spread_out + beside:
            copy.start()
        keep_a.start()

    @pl.when(s == 3)
    def _():
        for i in range(2):
            spread_out[i].wait_recv()
            pass_on[i].start()
            onward[i].start()

    @pl.loop(0, length // step)
    def _(t):
        sl = pl.ds(pl.multiple_of(t * step, step), step)
        v = x_ref[sl, :].astype(f32)
        a1_ref[sl, :] = (v * inverse_rms(v) * ag_ref[...]).astype(bf16)

    which = part_order(s)
    for half, p_ref in ((0, pa_ref), (1, pb_ref)):
        side = core if half == 0 else 1 - core
        if half:

            @pl.when(s == 0)
            def _():
                swap_p.wait_recv()
                keep_b.start()

        raw_ref[:, half * cols : (half + 1) * cols] = dot(a1_ref[...], p_ref[...])
        (q0, q1, k0), value = heads_of(
            raw_ref[:, half * cols : (half + 1) * cols], cos_ref[...], sin_ref[...], qg_ref[...], kg_ref[...]
        )
        for b in range(length // step):
            sl = slice(b * step, (b + 1) * step)
            span = (b + 1) * step
            qs = jnp.concatenate([q0[2][sl], q1[2][sl]], axis=0)
            probs = block_probs(qs, k0[2][:span], start_ref[sl, :], b * step, score_scale)
            mixed = dot(probs.astype(bf16), value[:span]).astype(bf16)
            for g in range(2):
                at = pl.ds(pl.multiple_of((2 * side + g) * HD, HD), HD)
                heads[which, sl, at] = mixed[g * step : (g + 1) * step]

    for at, k in enumerate(ORDER[:3]):

        @pl.when(s == at)
        def _():
            home[k - 1].start()

    @pl.when(s == 3)
    def _():
        mix[:, mine] = heads[0]
        for copy in pass_on:
            copy.wait_recv()
        onward[2].start()
        for copy in home:
            copy.wait_recv()
        for copy in beside + onward:
            copy.wait_recv()
        keep_out.start()

        @pl.loop(0, width // TILE)
        def _(t):
            sl = pl.ds(pl.multiple_of(t * TILE, TILE), TILE)
            after_ref[:, sl] = x_ref[:, sl].astype(f32) + dot(mix[...], wo[:, sl])

        @pl.loop(0, length // step)
        def _(t):
            sl = pl.ds(pl.multiple_of(t * step, step), step)
            v = after_ref[sl, :]
            inverse = inverse_rms(v)
            inv_ref[sl, :] = inverse
            a2[0, sl, :] = (v * inverse * mg_ref[...]).astype(bf16)

        a2_x.start()
        a2_y.start()
        keep[0].start()
        mixed_ref[...] = mix[...]
        a2_x.wait_recv()
        a2_high.start()
        keep[1].start()
        a2_y.wait_recv()
        a2_low.start()
        keep[2].start()
        a2_high.wait_recv()
        a2_low.wait_recv()
        keep[3].start()
        for copy in spread_out + pass_on + beside + onward + home + [a2_x, a2_y, a2_low, a2_high]:
            copy.wait_send()
        swap_p.wait_send()
        for copy in keep + [keep_out, keep_a, keep_b]:
            copy.wait()


def attend_forward(x, cosine, sine, starts, ag, mg, qg, kg, weights, depth, proj, length):
    tokens, width = x.shape
    planes = weights.shape[0]
    total = planes * depth
    anywhere = pl.BlockSpec(memory_space=pl.ANY)

    def in_order(cols):
        return pl.BlockSpec((length, cols), lambda s: (part_order(s), 0))

    return pl.pallas_call(
        attend_kernel,
        grid=(TP,),
        in_specs=[in_order(width)]
        + [in_order(HD), in_order(HD), in_order(1)]
        + [whole_spec(g.shape) for g in (ag, mg, qg, kg)]
        + [anywhere],
        out_specs=[in_order(8 * HD), in_order(width)]
        + [whole_spec((length, width))] * 2
        + [whole_spec((length, 1))]
        + [anywhere] * 4,
        out_shape=[
            struct((tokens, 8 * HD), f32),
            struct((tokens, width), bf16),
            struct((length, width), bf16),
            struct((length, width), f32),
            struct((length, 1), f32),
            struct((total, proj), bf16),
            struct((total, proj), bf16),
            struct((total, width), bf16),
            struct((tokens, width), bf16),
        ],
        scratch_shapes=[
            pltpu.VMEM((total, proj), bf16),
            pltpu.VMEM((total, proj), bf16),
            pltpu.SemaphoreType.DMA((planes, 2)),
            pltpu.VMEM((TP, length, 4 * HD), bf16),
            pltpu.VMEM((length, width), bf16),
            pltpu.VMEM((total, width), bf16),
            pltpu.VMEM((TP, length, width), bf16),
            pltpu.SemaphoreType.DMA,
            pltpu.SemaphoreType.DMA,
            pltpu.SemaphoreType.DMA((3,)),
            pltpu.SemaphoreType.DMA((3,)),
            pltpu.SemaphoreType.DMA((4,)),
            pltpu.SemaphoreType.DMA((4,)),
            pltpu.SemaphoreType.DMA((4,)),
            pltpu.SemaphoreType.DMA((4,)),
            pltpu.SemaphoreType.DMA((4,)),
            pltpu.SemaphoreType.DMA((4,)),
            pltpu.SemaphoreType.DMA((7,)),
        ],
        compiler_params=pltpu.CompilerParams(
            vmem_limit_bytes=56 << 20, collective_id=3, has_side_effects=True
        ),
        cost_estimate=pl.CostEstimate(
            flops=2 * tokens * width * 8 * HD, bytes_accessed=30 << 20, transcendentals=0
        ),
        name="attend_forward",
    )(x, cosine, sine, starts, ag, mg, qg, kg, weights)


def between_kernel(
    grad_ref, after_ref, inv_ref, gain_ref, cot_ref, w_ref,
    sum_ref, dy_ref, dgain_ref, heads_ref,
):
    length = after_ref.shape[0]
    step = 128

    @pl.when(pl.program_id(0) == 0)
    def _():
        dgain_ref[...] = jnp.zeros_like(dgain_ref)

        @pl.loop(0, length // step)
        def _(t):
            sl = pl.ds(pl.multiple_of(t * step, step), step)
            grad, values, inverse = grad_ref[sl, :], after_ref[sl, :], inv_ref[sl, :]
            scaled = grad * gain_ref[...]
            inner = jnp.mean(scaled * values, axis=-1, keepdims=True)
            total = cot_ref[sl, :].astype(f32) + inverse * (scaled - values * inverse * inverse * inner)
            sum_ref[sl, :] = total
            dy_ref[sl, :] = total.astype(bf16)
            dgain_ref[...] += jnp.sum(grad * values * inverse, axis=0, keepdims=True)

    heads_ref[...] = dot_nt(dy_ref[...], w_ref[...]).astype(bf16)


def between(grad, after, inverse, gain, cot, w):
    length, width = after.shape
    block = 256

    def once(v):
        return pl.BlockSpec(v.shape, lambda s: (0, 0), pipeline_mode=pl.Buffered(1))

    return pl.pallas_call(
        between_kernel,
        grid=(w.shape[0] // block,),
        in_specs=[once(v) for v in (grad, after, inverse, gain, cot)]
        + [pl.BlockSpec((block, width), lambda s: (s, 0))],
        out_specs=[whole_spec((length, width))] * 2
        + [whole_spec((1, width)), pl.BlockSpec((length, block), lambda s: (0, s))],
        out_shape=[
            struct((length, width), f32),
            struct((length, width), bf16),
            struct((1, width), f32),
            struct((length, w.shape[0]), bf16),
        ],
        compiler_params=pltpu.CompilerParams(vmem_limit_bytes=60 << 20),
        cost_estimate=pl.CostEstimate(
            flops=2 * length * width * w.shape[0], bytes_accessed=24 << 20, transcendentals=0
        ),
        name="between",
    )(grad, after, inverse, gain, cot, w)


def attend_backward(gm, raw, a1, pa, pb, cosine, sine, starts, qg, kg, mix, dy, length):
    tokens, width = a1.shape
    block = width // (2 * TP)
    anywhere = pl.BlockSpec(memory_space=pl.ANY)
    sem = pltpu.SemaphoreType.DMA

    def in_order(cols):
        return pl.BlockSpec((length, cols), lambda s: (part_order(s), 0))

    def once(v):
        return pl.BlockSpec(v.shape, lambda s: (0, 0), pipeline_mode=pl.Buffered(1))

    return pl.pallas_call(
        attend_back_kernel,
        grid=(TP,),
        in_specs=[anywhere]
        + [in_order(c) for c in (8 * HD, width)]
        + [once(w) for w in (pa, pb)]
        + [in_order(HD), in_order(HD), in_order(1)]
        + [whole_spec(v.shape) for v in (qg, kg)]
        + [once(v) for v in (mix, dy)],
        out_specs=[whole_spec((length, width)), whole_spec((width, pa.shape[1] + block))]
        + [whole_spec(v.shape) for v in (qg, kg)]
        + [anywhere] * 2,
        out_shape=[struct((length, width), f32), struct((width, pa.shape[1] + block), bf16)]
        + [struct(v.shape, f32) for v in (qg, kg)]
        + [struct((3, width, block), bf16), struct((TP, width, block), bf16)],
        scratch_shapes=[
            pltpu.VMEM((length, 8 * HD), bf16),
            pltpu.VMEM((length, HD), f32),
            pltpu.VMEM((length, HD), f32),
            pltpu.VMEM(pa.shape, f32),
            pltpu.VMEM(pa.shape, f32),
            pltpu.VMEM((TP, length, 4 * HD), bf16),
            pltpu.VMEM(pa.shape, bf16),
            pltpu.VMEM(pa.shape, bf16),
            pltpu.VMEM((TP, width, block), bf16),
            pltpu.VMEM((width, block), bf16),
        ]
        + scatter_scratch(length, width)
        + [sem((3,)), sem((3,)), sem, sem, sem, sem((TP,)), sem((TP,)), sem((4,)), sem((4,)), sem((TP,))],
        compiler_params=pltpu.CompilerParams(
            vmem_limit_bytes=60 << 20, collective_id=2, has_side_effects=True
        ),
        cost_estimate=pl.CostEstimate(
            flops=2 * tokens * width * 8 * HD, bytes_accessed=30 << 20, transcendentals=0
        ),
        name="attend_backward",
    )(gm, raw, a1, pa, pb, cosine, sine, starts, qg, kg, mix, dy)[:4]


def down_kernel(
    run, hid_ref, da_ref, db_ref, after_ref, rows_ref, gains_ref, near_ref, back_ref, x_ref, ag_ref, down_ref,
    out_ref, gate_ref, up_ref, total_ref, tokens_ref, wide_ref,
    hid, da, db, after, acc, pieces, gains, near, back, xs, down, loads, p_send, p_recv, g_send, g_recv,
    ebuf, rd, rxy, rs_send, rs_recv,
):
    length = after.shape[0]
    fn = da.shape[0]
    size, rows, _ = pieces.shape
    me = lax.axis_index("dp")
    x, y, _, _ = partners(me)
    others = everyone(me)
    scatter = Scatter(acc, ebuf, rd, rxy, rs_send, rs_recv, x, y)

    def block(device):
        return rows_ref.at[pl.ds(pl.multiple_of((device % size) * rows, rows), rows)]

    own = pltpu.make_async_copy(block(me), pieces.at[me % size], loads.at[0])
    copies = [
        remote(block(device), pieces.at[me % size], p_send.at[i], p_recv.at[i], device)
        for i, device in enumerate(others)
    ]
    own_gains = pltpu.make_async_copy(gains_ref.at[me % size], gains.at[me % size], loads.at[5])
    gain_copies = [
        remote(gains_ref.at[device % size], gains.at[me % size], g_send.at[i], g_recv.at[i], device)
        for i, device in enumerate(others)
    ]
    fills = [
        pltpu.make_async_copy(src, dst, loads.at[1 + i])
        for i, (src, dst) in enumerate(((hid_ref, hid), (da_ref, da), (db_ref, db), (after_ref, after)))
    ]
    extra = [
        pltpu.make_async_copy(near_ref, near, loads.at[6]),
        pltpu.make_async_copy(back_ref, back, loads.at[7]),
        pltpu.make_async_copy(x_ref, xs, loads.at[8]),
        pltpu.make_async_copy(down_ref, down, loads.at[9]),
    ]
    for copy in fills:
        copy.start()
    own.start()
    own_gains.start()
    for copy in extra:
        copy.start()
    greet(others)
    for copy in gain_copies:
        copy.start()
    for copy in fills:
        copy.wait()

    def part_of(k):
        sl = slice(k * length, (k + 1) * length)

        def tile_of(cut):
            value = dot(hid[sl, :fn], da[:, cut]) + dot(hid[sl, fn:], db[:, cut])
            return value + after[:, cut] if k == 0 else value

        return tile_of

    for k in ORDER[:3]:
        scatter.add(k, part_of(k))
    for copy in copies:
        copy.start()
    scatter.add(0, part_of(0))
    for copy in extra:
        copy.wait()

    step = 128

    @pl.loop(0, length // step)
    def _(t):
        sl = pl.ds(pl.multiple_of(t * step, step), step)
        values = xs[sl, :].astype(f32)
        inverse = inverse_rms(values)
        scaled = back[sl, :] * ag_ref[...]
        inner = jnp.mean(scaled * values, axis=-1, keepdims=True)
        tokens_ref[sl, :] = (
            near[sl, :] + inverse * (scaled - values * inverse * inverse * inner)
        ).astype(bf16)

    wide_ref[...] = down[...].astype(f32)
    own_gains.wait()
    for copy in gain_copies:
        copy.wait()
    total = jnp.sum(gains[...], axis=0)
    for g in range(total.shape[0]):
        total_ref[g] = total[g : g + 1]
    own.wait()
    for copy in copies:
        copy.wait()
    for source in range(size):
        piece = pieces[source].astype(f32)
        for g in range(fn // run):
            to = (g * size + source) * run
            gate_ref[:, to : to + run] = piece[:, g * run : (g + 1) * run]
            up_ref[:, to : to + run] = piece[:, fn + g * run : fn + (g + 1) * run]
    scatter.finish()
    out_ref[...] = acc[...].astype(bf16)


def down_forward(hid, da, db, after, mlp_rows, gains, near, back, x, ag, down, run):
    length, width = after.shape
    size = 2 * TP
    rows, cols = mlp_rows.shape[0] // size, mlp_rows.shape[1]
    ff = size * cols // 2
    anywhere = pl.BlockSpec(memory_space=pl.ANY)
    vmem = pl.BlockSpec(memory_space=pltpu.VMEM)
    sem = pltpu.SemaphoreType.DMA
    return pl.pallas_call(
        functools.partial(down_kernel, run),
        in_specs=[anywhere] * 9 + [vmem, anywhere],
        out_specs=[vmem] * 6,
        out_shape=[
            struct((length, width), bf16),
            struct((rows, ff), f32),
            struct((rows, ff), f32),
            struct((gains.shape[1], 1, gains.shape[2]), f32),
            struct((length, width), bf16),
            struct(down.shape, f32),
        ],
        scratch_shapes=[
            pltpu.VMEM(hid.shape, bf16),
            pltpu.VMEM(da.shape, bf16),
            pltpu.VMEM(db.shape, bf16),
            pltpu.VMEM(after.shape, f32),
            pltpu.VMEM(after.shape, f32),
            pltpu.VMEM((size, rows, cols), bf16),
            pltpu.VMEM(gains.shape, f32),
            pltpu.VMEM(after.shape, f32),
            pltpu.VMEM(after.shape, f32),
            pltpu.VMEM(x.shape, bf16),
            pltpu.VMEM(down.shape, bf16),
            sem((10,)), sem((size - 1,)), sem((size - 1,)), sem((size - 1,)), sem((size - 1,)),
        ]
        + scatter_scratch(length, width),
        compiler_params=pltpu.CompilerParams(
            vmem_limit_bytes=56 << 20, collective_id=7, has_side_effects=True
        ),
        cost_estimate=pl.CostEstimate(
            flops=2 * length * width * cols, bytes_accessed=30 << 20, transcendentals=0
        ),
        name="down_forward",
    )(hid, da, db, after, mlp_rows, gains, near, back, x, ag, down)


def return_kernel(
    rows_ref, gains_ref, q_ref, k_ref, v_ref, o_ref, total_ref, pieces, gains, send, recv, local, g_send, g_recv,
):
    size, rows, _ = pieces.shape
    me = lax.axis_index("dp")
    others = everyone(me)

    def block(device):
        return rows_ref.at[pl.ds(pl.multiple_of((device % size) * rows, rows), rows)]

    planes = gains.shape[0]
    plane = me // size
    column = [(plane + i) % planes for i in range(1, planes)]
    own = [
        pltpu.make_async_copy(block(me), pieces.at[me % size], local.at[0]),
        pltpu.make_async_copy(gains_ref.at[plane], gains.at[plane], local.at[1]),
    ]
    copies = [
        remote(block(device), pieces.at[me % size], send.at[i], recv.at[i], device)
        for i, device in enumerate(others)
    ]
    copies += [
        remote(gains_ref.at[to], gains.at[plane], g_send.at[i], g_recv.at[i], to * size + me % size)
        for i, to in enumerate(column)
    ]
    for copy in own:
        copy.start()
    greet(others + [to * size + me % size for to in column])
    for copy in copies:
        copy.start()
    for copy in own + copies:
        copy.wait()
    total_ref[...] = jnp.sum(gains[...], axis=0)
    for source in range(size):
        at = 0
        for ref in (q_ref, k_ref, v_ref, o_ref):
            width = ref.shape[1] // size
            ref[:, source * width : (source + 1) * width] = pieces[source, :, at : at + width].astype(f32)
            at += width


def return_attention(attn_rows, gains, widths):
    size = 2 * TP
    rows, cols = attn_rows.shape[0] // size, attn_rows.shape[1]
    sem = pltpu.SemaphoreType.DMA
    return pl.pallas_call(
        return_kernel,
        in_specs=[pl.BlockSpec(memory_space=pl.ANY)] * 2,
        out_specs=[pl.BlockSpec(memory_space=pltpu.VMEM)] * 5,
        out_shape=[struct((rows, w), f32) for w in widths] + [struct(gains.shape[1:], f32)],
        scratch_shapes=[
            pltpu.VMEM((size, rows, cols), bf16),
            pltpu.VMEM(gains.shape, f32),
            sem((size - 1,)), sem((size - 1,)), sem((2,)),
            sem((gains.shape[0] - 1,)), sem((gains.shape[0] - 1,)),
        ],
        compiler_params=pltpu.CompilerParams(collective_id=8, has_side_effects=True),
        name="return_attention",
    )(attn_rows, gains)


def make_body(n):
    m = n // (2 * TP)
    z_groups = [[g * 2 * TP + k for g in range(m)] for k in range(2 * TP)]

    def swap(v, bits):
        return lax.ppermute(v, "dp", [(a, a ^ bits) for a in range(n)])

    def gather_xy(v):
        h = v.shape[0] // 2
        x = swap(v, 2)
        y = swap(v, 4)
        d_low = swap(y[:h], 2)
        d_high = swap(x[h:], 4)
        return [v, x, y, jnp.concatenate([d_low, d_high])]

    def scatter_xy(p0, p1, p2, p3):
        h = p3.shape[0] // 2
        d_low = swap(p3[:h], 4)
        d_high = swap(p3[h:], 2)
        sx = jnp.concatenate([(p1[:h].astype(f32) + d_low.astype(f32)).astype(bf16), p1[h:]])
        sy = jnp.concatenate([p2[:h], (p2[h:].astype(f32) + d_high.astype(f32)).astype(bf16)])
        return p0 + swap(sx, 2).astype(f32) + swap(sy, 4).astype(f32)

    def gather_z(v):
        return lax.all_gather(v, "dp", axis=0, tiled=True, axis_index_groups=z_groups)

    def scatter_z(v):
        return lax.psum_scatter(
            v, "dp", scatter_dimension=0, tiled=True, axis_index_groups=z_groups
        )

    def body(
        tokens,
        segments,
        w_query,
        w_key,
        w_value,
        w_out,
        w_gate,
        w_up,
        w_down,
        attn_gain,
        mlp_gain,
        query_gain,
        key_gain,
        cotangent,
    ):
        me = lax.axis_index("dp")
        core = me % 2
        place = (me // 2) % TP
        length, width = tokens.shape
        rows = w_query.shape[0]
        ffr = w_down.shape[0]

        qn = w_query.shape[1] // (2 * TP)
        kn = w_key.shape[1] // (2 * TP)
        pn = qn + 2 * kn
        hr = query_gain.shape[0]
        gains = jnp.concatenate([attn_gain, mlp_gain, query_gain, key_gain]).astype(f32)
        count = gains.shape[0]
        padded = -(-count // 256) * 256
        attn_in, gains, seg_all = spread_attention(
            w_query, w_key, w_value, w_out, jnp.pad(gains, (0, padded - count))[None], segments
        )

        depth, wide = attn_in.shape
        gain_rows = gains.astype(bf16).reshape(-1, padded)
        below = jnp.pad(gain_rows, ((0, -gain_rows.shape[0] % 16), (0, wide - padded)))
        attn_all = gather_z(jnp.concatenate([attn_in, below])).reshape(m, -1, wide)
        tokens_in, _ = lax.optimization_barrier((tokens, attn_in))

        rate = THETA ** (-(jnp.arange(HD // 2, dtype=f32) * 2.0 / HD))
        sign = jnp.where(jnp.arange(HD) < HD // 2, -1.0, 1.0).astype(f32)
        rates = jnp.stack([jnp.concatenate([rate, rate]), sign])
        cosine, sine, starts, tokens_all, mlp_in = gather_group(
            seg_all, rates, tokens_in, w_gate, w_up, ffr
        )
        mlp_a = gather_z(mlp_in)
        tokens_all, attn_all = lax.optimization_barrier((tokens_all, attn_all))
        gains = attn_all[:, depth : depth + gain_rows.shape[0], :padded].reshape(n, padded)
        attn_scale = gains[:, :rows].reshape(-1).astype(f32)
        mlp_scale = gains[:, rows : 2 * rows].reshape(-1).astype(f32)
        query_scale = gains[:, 2 * rows : 2 * rows + hr].reshape(-1).astype(f32)
        key_scale = gains[:, 2 * rows + hr : count].reshape(-1).astype(f32)

        (
            raw, normed_one, mixed_own, after_attn, inv_two, proj_a, proj_b, out_full, normed_two_all
        ) = attend_forward(
            tokens_all, cosine, sine, starts, attn_scale[None], mlp_scale[None],
            query_scale[None], key_scale[None], attn_all, depth, pn, length,
        )

        inputs = tokens.astype(f32)
        mlp_a, normed_two_all, down_local = lax.optimization_barrier((mlp_a, normed_two_all, w_down))
        down_a = gather_z(down_local)
        fn = down_a.shape[0]

        gate_value, up_value, hidden, mlp_b, grad_all, down_sum = feed_forward(
            normed_two_all, mlp_a, cotangent
        )
        down_rows = scatter_z(down_sum)
        grad_normed_two, mlp_sum, down_b = feed_backward(
            gate_value, up_value, grad_all, down_a, mlp_a, mlp_b, normed_two_all, length
        )
        mlp_rows = scatter_z(mlp_sum)
        grad_normed_two, down_rows = lax.optimization_barrier((grad_normed_two, down_rows))

        grad_after, grad_after_low, mlp_gain_grad, grad_mixed = between(
            grad_normed_two, after_attn, inv_two, mlp_scale[None], cotangent, out_full
        )

        grad_normed_one, attn_sum, query_gain_grad, key_gain_grad = attend_backward(
            grad_mixed, raw, normed_one, proj_a, proj_b, cosine, sine, starts,
            query_scale[None], key_scale[None], mixed_own, grad_after_low, length,
        )
        attn_rows = scatter_z(attn_sum)
        attn_gain_grad = jnp.sum(grad_normed_one * inputs * inverse_rms(inputs), axis=0)

        gain_grads = jnp.concatenate(
            [
                attn_gain_grad.reshape(m, 2 * TP, -1),
                mlp_gain_grad.reshape(m, 2 * TP, -1),
                query_gain_grad.reshape(m, 2 * TP, -1),
                key_gain_grad.reshape(m, 2 * TP, -1),
                jnp.zeros((m, 2 * TP, padded - count), f32),
            ],
            axis=2,
        ).transpose(1, 0, 2)
        output, gate_shard, up_shard, gain_sums, tokens_grad, down_shard = down_forward(
            hidden, down_a, down_b, after_attn, mlp_rows, gain_grads, grad_after, grad_normed_one,
            tokens, attn_scale[None], down_rows, ffr,
        )
        attn_rows, output = lax.optimization_barrier((attn_rows, output))
        query_shard, key_shard, value_shard, out_shard, gain_grads = return_attention(
            attn_rows, gain_sums, [w.shape[1] for w in (w_query, w_key, w_value, w_out)]
        )

        gain_grads = gain_grads[0]

        return (
            output,
            tokens_grad,
            query_shard,
            key_shard,
            value_shard,
            out_shard,
            gate_shard,
            up_shard,
            down_shard,
            gain_grads[:rows],
            gain_grads[rows : 2 * rows],
            gain_grads[2 * rows : 2 * rows + hr],
            gain_grads[2 * rows + hr : count],
        )

    return body


def solution(mesh):
    row = P("dp", None)
    flat = P("dp")
    return jax.shard_map(
        make_body(mesh.shape["dp"]),
        mesh=mesh,
        in_specs=(row,) * 9 + (flat,) * 4 + (row,),
        out_specs=(row,) * 9 + (flat,) * 4,
        check_vma=False,
    )
```

profile of v0, /device:TPU:1, one launch (start us, length us, event | category | flops | bytes accessed | tf_op | source)
XLA Modules:
  0.0 636.1 jit_solution(13814705626244362362)
XLA Ops:
  7.2 0.0 all-gather.6.cloned.1.call-start
  7.2 1.3 fusion.12
  8.6 14.8 %spread_attention.1 = (bf16[512,768]{1,0:T(8,128)(2,1)}, f32[8,1,256]{2,1,0:T(1,128)}, s32[4,1,384]{2,1,0:T(1,128)}) custom-call(bf16[64,2048]{1,0:T(8,128)(2,1)} %wq_ref.1, bf16[64,1024]{1,0:T(8,128)(2,1)} %wk_ref.1, bf16[64,1024]{1,0:T(8,128)(2,1)} %wv_ref.1, bf16[64,2048]{1,0:T(8,128)(2,1)} %wo_ref.1, f32[1,256]{1,0:T(1,128)} %bitcast.20, s32[1,384]{1,0:T(1,128)} %seg_ref.1), custom_call_target="tpu_custom_call" | custom-call | tf_op jit(solution)/shard_map/spread_attention/pallas_call | solution.py:831
  23.3 0.7 convert_element_type.63
  24.1 2.1 fusion.4
  26.1 0.0 all-gather.6.cloned.1.call-update
  26.1 0.0 all-gather.4.cloned.1.call-start
  26.2 0.1 maximum_bitcast_fusion
  26.3 0.6 pad_maximum_fusion.rate_ref
  26.9 73.5 %gather_group.1 = (f32[1536,128]{1,0:T(8,128)}, f32[1536,128]{1,0:T(8,128)}, s32[1536,1]{1,0:T(8,128)}, bf16[1536,2048]{1,0:T(8,128)(2,1)}, bf16[512,1536]{1,0:T(8,128)(2,1)}) custom-call(s32[4,1,384]{2,1,0:T(1,128)} %get-tuple-element.68.seg_ref, f32[2,128]{1,0:T(2,128)} %pad_maximum_fusion.rate_ref, bf16[384,2048]{1,0:T(8,128)(2,1)} %x_ref.2, ...), custom_call_target="tpu_custom_call" | custom-call | tf_op jit(solution)/shard_map/gather_group/pallas_call | solution.py:927
  100.3 0.0 all-gather.4.cloned.1.call-update
  100.4 0.0 all-gather.8.cloned.1.call-start
  100.4 0.0 all-gather.6.cloned.1.call-done
  100.4 0.7 slice_bitcast_fusion
  101.2 0.1 slice_convert_fusion.2
  101.2 0.7 reshape.129.ag_ref
  101.9 0.7 reshape.130.mg_ref.gain_ref
  102.6 0.1 slice_convert_fusion
  102.7 0.6 reshape.131.qg_ref
  103.3 0.6 reshape.132.kg_ref
  103.9 122.0 %attend_forward.1 = (f32[1536,1024]{1,0:T(8,128)}, bf16[1536,2048]{1,0:T(8,128)(2,1)}, bf16[384,2048]{1,0:T(8,128)(2,1)}, f32[384,2048]{1,0:T(8,128)}, f32[384,1...) custom-call(bf16[1536,2048]{1,0:T(8,128)(2,1)} %get-tuple-element.74, ...), custom_call_target="tpu_custom_call" | custom-call | flops 6442450944 | bytes 31457280 | tf_op jit(solution)/shard_map/attend_forward/pallas_call | solution.py:1133
  225.9 0.0 all-gather.4.cloned.1.call-done.wa_ref
  226.0 0.0 all-gather.8.cloned.1.call-update
  226.0 0.5 reduce-scatter.4.cloned.1.call-start
  226.5 63.7 %feed_forward.1 = (bf16[1536,1536]{1,0:T(8,128)(2,1)}, bf16[1536,1536]{1,0:T(8,128)(2,1)}, bf16[1536,1536]{1,0:T(8,128)(2,1)}, bf16[2048,1536]{1,0:T(8,128)(2,1)...) custom-call(bf16[1536,2048]{1,0:T(8,128)(2,1)} %get-tuple-element.80.a2_ref, ...), custom_call_target="tpu_custom_call" | custom-call | flops 9663676416 | bytes 31457280 | tf_op jit(solution)/shard_map/feed_forward/pallas_call | solution.py:525
  290.2 0.0 reduce-scatter.4.cloned.1.call-update
  290.2 0.0 reduce-scatter.8.cloned.1.call-start
  290.3 0.0 all-gather.8.cloned.1.call-done.da_ref
  290.3 83.4 %feed_backward.1 = (f32[384,2048]{1,0:T(8,128)}, bf16[2048,1536]{1,0:T(8,128)(2,1)}, bf16[768,2048]{1,0:T(8,128)(2,1)}, bf16[2048,1536]{1,0:T(8,128)(2,1)}) custom-call(bf16[1536,1536]{1,0:T(8,128)(2,1)} %get-tuple-element.82.gate_ref, bf16[1536,1536]{1,0:T(8,128)(2,1)} %get-tuple-element.83.up_ref, bf16[1536,2048]{1,0:T(8,128)(2,1)} %get-tuple-element.84.ga_ref, ...), custom_call_target="tpu_custom_call" | custom-call | flops 19327352832 | bytes 31457280 | tf_op jit(solution)/shard_map/feed_backward/pallas_call | solution.py:716
  373.7 0.0 reduce-scatter.8.cloned.1.call-update
  373.7 0.0 reduce-scatter.6.cloned.1.call-start
  373.8 0.0 reduce-scatter.4.cloned.1.call-done.down_ref
  373.8 15.5 %between.1 = (f32[384,2048]{1,0:T(8,128)}, bf16[384,2048]{1,0:T(8,128)(2,1)}, f32[1,2048]{1,0:T(1,128)}, bf16[384,2048]{1,0:T(8,128)(2,1)}) custom-call(f32[384,2048]{1,0:T(8,128)} %get-tuple-element.89.grad_ref, f32[384,2048]{1,0:T(8,128)} %get-tuple-element.90.after_ref, f32[384,1]{1,0:T(8,128)} %get-tuple-element.91.inv_ref, ...), custom_call_target="tpu_custom_call" | custom-call | flops 3221225472 | bytes 25165824 | tf_op jit(solution)/shard_map/between/pallas_call | solution.py:1217
  389.3 116.0 %attend_backward.1 = (f32[384,2048]{1,0:T(8,128)}, bf16[2048,768]{1,0:T(8,128)(2,1)}, f32[1,128]{1,0:T(1,128)}, f32[1,128]{1,0:T(1,128)}, bf16[3,2048,256]{2,1,0:T(8,128)(2,1)}, /*index=5*/bf16[4,2048,256]{2,1,0:T(8,128)(2,1)}) custom-call(bf16[384,2048]{1,0:T(8,128)(2,1)} %get-tuple-element.93.gm_ref, f32[1536,1024]{1,0:T(8,128)} %get-tuple-element.94.raw_ref, ...), custom_call_target="tpu_custom_call" | custom-call | flops 6442450944 | bytes 31457280 | tf_op jit(solution)/shard_map/attend_backward/pallas_call | solution.py:1250
  505.2 0.0 copy-start
  505.2 0.0 reduce-scatter.6.cloned.1.call-update
  505.3 1.4 copy-done
  506.6 0.4 fusion.2
  507.0 2.3 fusion.1
  509.4 0.1 reshape.124
  509.5 0.5 broadcast.61
  510.0 0.0 copy-done.11
  510.0 0.7 reduce.10
  510.6 0.1 reshape.126
  510.8 0.7 reduce.11
  511.4 0.1 reshape.127
  511.5 0.0 copy-done.9
  511.6 0.7 reduce.9
  512.2 0.1 reshape.125
  512.3 0.7 concatenate.15
  513.1 83.3 %down_forward.1 = (bf16[384,2048]{1,0:T(8,128)(2,1)}, f32[64,6144]{1,0:T(8,128)}, f32[64,6144]{1,0:T(8,128)}, f32[4,1,256]{2,1,0:T(1,128)}, bf16[384,2048]{1,0:T(8,128)(2,1)}, /*index=5*/f32[192,2048]{1,0:T(8,128)}) custom-call(bf16[1536,1536]{1,0:T(8,128)(2,1)} %get-tuple-element.101.hid_ref, bf16[768,2048]{1,0:T(8,128)(2,1)} %all-gather.8.cloned.1.call-done.da_ref, ...), custom_call_target="tpu_custom_call" | custom-call | flops 2415919104 | bytes 31457280 | tf_op jit(solution)/shard_map/down_forward/pallas_call | solution.py:1396
  596.4 0.0 reduce-scatter.6.cloned.1.call-done.rows_ref
  596.4 19.3 %return_attention.1 = (f32[64,2048]{1,0:T(8,128)}, f32[64,1024]{1,0:T(8,128)}, f32[64,1024]{1,0:T(8,128)}, f32[64,2048]{1,0:T(8,128)}, f32[1,256]{1,0:T(1,128)}) custom-call(bf16[512,768]{1,0:T(8,128)(2,1)} %reduce-scatter.6.cloned.1.call-done.rows_ref, f32[4,1,256]{2,1,0:T(1,128)} %get-tuple-element.114.gains_ref), custom_call_target="tpu_custom_call" | custom-call | tf_op jit(solution)/shard_map/return_attention/pallas_call | solution.py:1478
  615.7 1.3 slice_bitcast_fusion.3
  617.0 1.3 slice_bitcast_fusion.1
  618.4 2.8 copy.45
  621.2 1.1 copy.46
  622.3 0.8 copy.47
  623.1 0.7 copy.48
  623.8 0.7 copy.49
  624.5 0.8 copy.50
  625.3 1.1 copy.51
  626.5 1.1 copy.52
  627.6 1.1 copy.53
  (30 shorter events, 0.1 us)
Async XLA Ops:
  7.2 93.2 %all-gather.6.cloned.1.call-start = ((), (), s32[]{:S(2)}) async-start(), calls=%async_computation.4 | async-start | bytes 4055040 | tf_op jit(solution)/shard_map/all_gather | solution.py:1518
  26.1 199.8 %all-gather.4.cloned.1.call-start = ((), (), s32[]{:S(2)}) async-start(), calls=%async_computation.3 | async-start | bytes 7864320 | tf_op jit(solution)/shard_map/all_gather | solution.py:1518
  100.4 189.9 %all-gather.8.cloned.1.call-start = ((), (), s32[]{:S(2)}) async-start(), calls=%async_computation.5 | async-start | bytes 3932160 | tf_op jit(solution)/shard_map/all_gather | solution.py:1518
  226.0 147.8 %reduce-scatter.4.cloned.1.call-start = ((), (), s32[]{:S(2)}) async-start(), calls=%async_computation.6 | async-start | bytes 3932160 | tf_op jit(solution)/shard_map/reduce_scatter | solution.py:1521
  290.2 222.8 %reduce-scatter.8.cloned.1.call-start = ((), (), s32[]{:S(2)}) async-start(), calls=%async_computation.8 | async-start | bytes 7864320 | tf_op jit(solution)/shard_map/reduce_scatter | solution.py:1521
  373.7 222.7 %reduce-scatter.6.cloned.1.call-start = ((), (), s32[]{:S(2)}) async-start(), calls=%async_computation.7 | async-start | bytes 3932160 | tf_op jit(solution)/shard_map/reduce_scatter | solution.py:1521
  505.2 1.4 copy-start
  506.6 3.3 copy-start.11
  506.6 4.1 copy-start.10
  506.6 4.9 copy-start.9
  596.4 24.8 %copy-start.4 = (bf16[384,2048]{1,0:T(8,128)(2,1)S(1)}, bf16[384,2048]{1,0:T(8,128)(2,1)}, u32[]{:S(2)}) copy-start(bf16[384,2048]{1,0:T(8,128)(2,1)} %get-tuple-element.145) | copy-start | bytes 4718596
  618.4 4.0 copy-start.6
  618.4 4.8 copy-start.8
  621.2 2.7 copy-start.7
  621.2 3.4 copy-start.5
  621.2 4.2 copy-start.3
  622.3 4.2 copy-start.2
  625.3 2.3 copy-start.1
Sparse Core Ops, SparseCore 0:
  26.3 65.9 all-gather.5
  100.5 115.9 all-gather.3
  226.1 63.2 all-gather.7
  291.5 58.7 reduce-scatter.3
  373.8 113.6 reduce-scatter.7
  505.4 65.1 reduce-scatter.5
where the time goes:
time: 644 us; the launch traced here: 636 us
  Pallas kernels  591 us (92%)
  local copies, waits for them, and re-layouts  19.4 us (3%)
  between operations  14.8 us (2%)
  other arithmetic  9.67 us (2%)
    pallas_call x1, Pallas kernels, attend_forward(): pl.pallas_call(attend_kernel, grid=(TP,), in_specs=[in_order(width)] + [i...  122 us
    pallas_call x1, Pallas kernels, attend_backward(): pl.pallas_call(attend_back_kernel, grid=(TP,), in_specs=[anywhere] + [in_...  116 us
    pallas_call x1, Pallas kernels, feed_backward(): pl.pallas_call(feed_back_kernel, in_specs=[anywhere] * 7, out_specs=[pl.B...  83.4 us
    pallas_call x1, Pallas kernels, down_forward(): pl.pallas_call(functools.partial(down_kernel, run), in_specs=[anywhere] *...  83.3 us
    pallas_call x1, Pallas kernels, gather_group(): pl.pallas_call(functools.partial(gather_kernel, run), in_specs=[vmem] * 2...  73.5 us
    pallas_call x1, Pallas kernels, feed_forward(): pl.pallas_call(feed_kernel, in_specs=[anywhere] * 3, out_specs=[anywhere]...  63.7 us
    pallas_call x1, Pallas kernels, return_attention(): pl.pallas_call(return_kernel, in_specs=[pl.BlockSpec(memory_space=pl.ANY)...  19.3 us
    pallas_call x1, Pallas kernels, between(): pl.pallas_call(between_kernel, grid=(w.shape[0] // block,), in_specs=[onc...  15.5 us
  transfers between devices with their start and end apart: 6, of which 0 were waited for; matrix products, arithmetic and copies ran while one was open for 2% of the time, Pallas kernels for 88%

commit v1 on v0

--- a/solution.py
+++ b/solution.py
@@ -171,11 +171,10 @@
 
 
 def attend_back_kernel(
-    gm_ref, raw_ref, a1_ref, pa_ref, pb_ref, cos_ref, sin_ref, start_ref, qg_ref, kg_ref, mix_ref, dy_ref,
-    out_ref, sum_ref, dqg_ref, dkg_ref, ogot_ref, orecv_ref,
-    gp_ref, dk_ref, dv_ref, acc_a, acc_b, heads, cbuf, crecv, oslot, ofetch,
-    ebuf, rd, rxy, rs_send, rs_recv, do_send, do_recv, do_own, c_send, c_recv,
-    oc_send, oc_recv, os_send, os_recv, o_local,
+    heads, raw_ref, a1_ref, pa_ref, pb_ref, cos_ref, sin_ref, start_ref, qg_ref, kg_ref, mix_ref, dy_ref, orecv_ref,
+    out_ref, sum_ref, dqg_ref, dkg_ref, ogot_ref,
+    gp_ref, dk_ref, dv_ref, acc_a, acc_b, cbuf, crecv, oslot, ofetch,
+    ebuf, rd, rxy, rs_send, rs_recv, c_send, c_recv, os_send, os_recv, o_local,
 ):
     length = a1_ref.shape[0]
     step = 128
@@ -183,26 +182,10 @@
     s = pl.program_id(0)
     me = lax.axis_index("dp")
     core = me % 2
-    place = (me // 2) % TP
     x, y, d, sibling = partners(me)
-    cols = 4 * HD
-
-    def columns_of(device):
-        return pl.ds(pl.multiple_of(((device // 2) % TP) * cols, cols), cols)
-
-    incoming = [
-        remote(gm_ref.at[:, columns_of(device)], heads.at[k], do_send.at[k - 1], do_recv.at[k - 1], device)
-        for k, device in ((1, x), (2, y), (3, d))
-    ]
-    own = pltpu.make_async_copy(
-        gm_ref.at[:, pl.ds(pl.multiple_of(place * cols, cols), cols)], heads.at[0], do_own
-    )
     scatter = Scatter(out_ref, ebuf, rd, rxy, rs_send, rs_recv, x, y)
     across = remote(cbuf, crecv, c_send, c_recv, sibling)
     block = oslot.shape[2]
-    o_across = [
-        remote(oslot.at[k], orecv_ref.at[k], oc_send.at[k], oc_recv.at[k], sibling) for k in range(TP)
-    ]
     tall = oslot.shape[1] // 2
     o_low = remote(
         oslot.at[3, pl.ds(0, tall)], ogot_ref.at[2, pl.ds(0, tall)], os_send.at[2], os_recv.at[2], y
@@ -229,26 +212,9 @@
     @pl.when(s == 0)
     def _():
         greet((x, y, d, sibling))
-        for k in (2, 0, 1):
-            incoming[k].start()
-        own.start()
         for ref in (acc_a, acc_b, dqg_ref, dkg_ref):
             ref[...] = jnp.zeros_like(ref)
         for k in (3, 1, 2, 0):
-
-            @pl.loop(0, oslot.shape[1] // TILE)
-            def _(t):
-                sl = pl.ds(pl.multiple_of(t * TILE, TILE), TILE)
-                oslot[k, sl, :] = out_tile(k, 1 - core, sl).astype(bf16)
-
-            o_across[k].start()
-        incoming[2].wait_recv()
-
-    @pl.when(s == 1)
-    def _():
-        for k in (3, 1, 2, 0):
-            o_across[k].wait_send()
-            o_across[k].wait_recv()
             fetch = pltpu.make_async_copy(orecv_ref.at[k], ofetch, o_local.at[0])
             fetch.start()
             fetch.wait()
@@ -261,9 +227,8 @@
             if k == 3:
                 o_low.start()
                 o_high.start()
-        incoming[0].wait_recv()
-
-    @pl.when(s == 2)
+
+    @pl.when(s == 1)
     def _():
         for copy, k, offset in ((o_low, 1, 0), (o_high, 2, tall)):
             copy.wait_recv()
@@ -280,11 +245,6 @@
                 oslot[k, to, :] = (oslot[k, to, :].astype(f32) + ofetch[sl, :].astype(f32)).astype(bf16)
 
             o_home[k - 1].start()
-        incoming[1].wait_recv()
-
-    @pl.when(s == 3)
-    def _():
-        own.wait()
 
     which = part_order(s)
 
@@ -382,8 +342,6 @@
 
         scatter.finish()
         across.wait_send()
-        for copy in incoming:
-            copy.wait_send()
 
 
 CHUNK = 256
@@ -1183,59 +1141,111 @@
 
 
 def between_kernel(
-    grad_ref, after_ref, inv_ref, gain_ref, cot_ref, w_ref,
-    sum_ref, dy_ref, dgain_ref, heads_ref,
+    grad_ref, after_ref, inv_ref, gain_ref, cot_ref, mix_ref, w_ref,
+    sum_ref, dy_ref, dgain_ref, heads_ref, orecv_ref,
+    w, heads, oslot, loads, h_send, h_recv, o_send, o_recv,
 ):
-    length = after_ref.shape[0]
+    length, width = after_ref.shape
     step = 128
-
-    @pl.when(pl.program_id(0) == 0)
-    def _():
-        dgain_ref[...] = jnp.zeros_like(dgain_ref)
-
-        @pl.loop(0, length // step)
+    me = lax.axis_index("dp")
+    core = me % 2
+    x, y, d, sibling = partners(me)
+    places = (me, x, y, d)
+    cols = heads.shape[2]
+    block = oslot.shape[2]
+
+    def rows_of(device):
+        return pl.ds(pl.multiple_of(((device // 2) % TP) * cols, cols), cols)
+
+    load = [
+        pltpu.make_async_copy(w_ref.at[rows_of(device)], w.at[k], loads.at[k])
+        for k, device in enumerate(places)
+    ]
+    home = [
+        remote(heads.at[k], heads_ref.at[k], h_send.at[k - 1], h_recv.at[k - 1], places[k])
+        for k in range(1, TP)
+    ]
+    keep = pltpu.make_async_copy(heads.at[0], heads_ref.at[0], loads.at[TP])
+    across = [
+        remote(oslot.at[k], orecv_ref.at[k], o_send.at[k], o_recv.at[k], sibling) for k in range(TP)
+    ]
+    for k in ORDER:
+        load[k].start()
+    greet((x, y, d, sibling))
+    dgain_ref[...] = jnp.zeros_like(dgain_ref)
+
+    @pl.loop(0, length // step)
+    def _(t):
+        sl = pl.ds(pl.multiple_of(t * step, step), step)
+        grad, values, inverse = grad_ref[sl, :], after_ref[sl, :], inv_ref[sl, :]
+        scaled = grad * gain_ref[...]
+        inner = jnp.mean(scaled * values, axis=-1, keepdims=True)
+        total = cot_ref[sl, :].astype(f32) + inverse * (scaled - values * inverse * inverse * inner)
+        sum_ref[sl, :] = total
+        dy_ref[sl, :] = total.astype(bf16)
+        dgain_ref[...] += jnp.sum(grad * values * inverse, axis=0, keepdims=True)
+
+    def out_half(k):
+        at = ((places[k] // 2) % TP) * 2 + 1 - core
+        cut = pl.ds(pl.multiple_of(at * block, block), block)
+
+        @pl.loop(0, oslot.shape[1] // TILE)
         def _(t):
-            sl = pl.ds(pl.multiple_of(t * step, step), step)
-            grad, values, inverse = grad_ref[sl, :], after_ref[sl, :], inv_ref[sl, :]
-            scaled = grad * gain_ref[...]
-            inner = jnp.mean(scaled * values, axis=-1, keepdims=True)
-            total = cot_ref[sl, :].astype(f32) + inverse * (scaled - values * inverse * inverse * inner)
-            sum_ref[sl, :] = total
-            dy_ref[sl, :] = total.astype(bf16)
-            dgain_ref[...] += jnp.sum(grad * values * inverse, axis=0, keepdims=True)
-
-    heads_ref[...] = dot_nt(dy_ref[...], w_ref[...]).astype(bf16)
-
-
-def between(grad, after, inverse, gain, cot, w):
+            sl = pl.ds(pl.multiple_of(t * TILE, TILE), TILE)
+            oslot[k, sl, :] = dot_tn(mix_ref[:, sl], dy_ref[:, cut]).astype(bf16)
+
+        across[k].start()
+
+    out_half(3)
+    for k in ORDER:
+        load[k].wait()
+        heads[k] = dot_nt(dy_ref[...], w[k]).astype(bf16)
+        if k:
+            home[k - 1].start()
+        else:
+            keep.start()
+    for k in ORDER[1:]:
+        out_half(k)
+    for copy in home + across:
+        copy.wait()
+    keep.wait()
+
+
+def between(grad, after, inverse, gain, cot, mix, w):
     length, width = after.shape
-    block = 256
-
-    def once(v):
-        return pl.BlockSpec(v.shape, lambda s: (0, 0), pipeline_mode=pl.Buffered(1))
-
+    cols = w.shape[0] // TP
+    block = width // (2 * TP)
+    anywhere = pl.BlockSpec(memory_space=pl.ANY)
+    vmem = pl.BlockSpec(memory_space=pltpu.VMEM)
+    sem = pltpu.SemaphoreType.DMA
     return pl.pallas_call(
         between_kernel,
-        grid=(w.shape[0] // block,),
-        in_specs=[once(v) for v in (grad, after, inverse, gain, cot)]
-        + [pl.BlockSpec((block, width), lambda s: (s, 0))],
-        out_specs=[whole_spec((length, width))] * 2
-        + [whole_spec((1, width)), pl.BlockSpec((length, block), lambda s: (0, s))],
+        in_specs=[vmem] * 6 + [anywhere],
+        out_specs=[vmem] * 3 + [anywhere] * 2,
         out_shape=[
             struct((length, width), f32),
             struct((length, width), bf16),
             struct((1, width), f32),
-            struct((length, w.shape[0]), bf16),
+            struct((TP, length, cols), bf16),
+            struct((TP, width, block), bf16),
         ],
-        compiler_params=pltpu.CompilerParams(vmem_limit_bytes=60 << 20),
+        scratch_shapes=[
+            pltpu.VMEM((TP, cols, width), bf16),
+            pltpu.VMEM((TP, length, cols), bf16),
+            pltpu.VMEM((TP, width, block), bf16),
+            sem((TP + 1,)), sem((3,)), sem((3,)), sem((TP,)), sem((TP,)),
+        ],
+        compiler_params=pltpu.CompilerParams(
+            vmem_limit_bytes=60 << 20, collective_id=9, has_side_effects=True
+        ),
         cost_estimate=pl.CostEstimate(
-            flops=2 * length * width * w.shape[0], bytes_accessed=24 << 20, transcendentals=0
+            flops=4 * length * width * w.shape[0], bytes_accessed=24 << 20, transcendentals=0
         ),
         name="between",
-    )(grad, after, inverse, gain, cot, w)
-
-
-def attend_backward(gm, raw, a1, pa, pb, cosine, sine, starts, qg, kg, mix, dy, length):
+    )(grad, after, inverse, gain, cot, mix, w)
+
+
+def attend_backward(heads, raw, a1, pa, pb, cosine, sine, starts, qg, kg, mix, dy, orecv, length):
     tokens, width = a1.shape
     block = width // (2 * TP)
     anywhere = pl.BlockSpec(memory_space=pl.ANY)
@@ -1250,32 +1260,32 @@
     return pl.pallas_call(
         attend_back_kernel,
         grid=(TP,),
-        in_specs=[anywhere]
+        in_specs=[pl.BlockSpec(heads.shape, lambda s: (0, 0, 0), pipeline_mode=pl.Buffered(1))]
         + [in_order(c) for c in (8 * HD, width)]
         + [once(w) for w in (pa, pb)]
         + [in_order(HD), in_order(HD), in_order(1)]
         + [whole_spec(v.shape) for v in (qg, kg)]
-        + [once(v) for v in (mix, dy)],
+        + [once(v) for v in (mix, dy)]
+        + [anywhere],
         out_specs=[whole_spec((length, width)), whole_spec((width, pa.shape[1] + block))]
         + [whole_spec(v.shape) for v in (qg, kg)]
-        + [anywhere] * 2,
+        + [anywhere],
         out_shape=[struct((length, width), f32), struct((width, pa.shape[1] + block), bf16)]
         + [struct(v.shape, f32) for v in (qg, kg)]
-        + [struct((3, width, block), bf16), struct((TP, width, block), bf16)],
+        + [struct((3, width, block), bf16)],
         scratch_shapes=[
             pltpu.VMEM((length, 8 * HD), bf16),
             pltpu.VMEM((length, HD), f32),
             pltpu.VMEM((length, HD), f32),
             pltpu.VMEM(pa.shape, f32),
             pltpu.VMEM(pa.shape, f32),
-            pltpu.VMEM((TP, length, 4 * HD), bf16),
             pltpu.VMEM(pa.shape, bf16),
             pltpu.VMEM(pa.shape, bf16),
             pltpu.VMEM((TP, width, block), bf16),
             pltpu.VMEM((width, block), bf16),
         ]
         + scatter_scratch(length, width)
-        + [sem((3,)), sem((3,)), sem, sem, sem, sem((TP,)), sem((TP,)), sem((4,)), sem((4,)), sem((TP,))],
+        + [sem, sem, sem((4,)), sem((4,)), sem((TP,))],
         compiler_params=pltpu.CompilerParams(
             vmem_limit_bytes=60 << 20, collective_id=2, has_side_effects=True
         ),
@@ -1283,7 +1293,7 @@
             flops=2 * tokens * width * 8 * HD, bytes_accessed=30 << 20, transcendentals=0
         ),
         name="attend_backward",
-    )(gm, raw, a1, pa, pb, cosine, sine, starts, qg, kg, mix, dy)[:4]
+    )(heads, raw, a1, pa, pb, cosine, sine, starts, qg, kg, mix, dy, orecv)[:4]
 
 
 def down_kernel(
@@ -1598,13 +1608,13 @@
         mlp_rows = scatter_z(mlp_sum)
         grad_normed_two, down_rows = lax.optimization_barrier((grad_normed_two, down_rows))
 
-        grad_after, grad_after_low, mlp_gain_grad, grad_mixed = between(
-            grad_normed_two, after_attn, inv_two, mlp_scale[None], cotangent, out_full
+        grad_after, grad_after_low, mlp_gain_grad, grad_heads, out_other = between(
+            grad_normed_two, after_attn, inv_two, mlp_scale[None], cotangent, mixed_own, out_full
         )
 
         grad_normed_one, attn_sum, query_gain_grad, key_gain_grad = attend_backward(
-            grad_mixed, raw, normed_one, proj_a, proj_b, cosine, sine, starts,
-            query_scale[None], key_scale[None], mixed_own, grad_after_low, length,
+            grad_heads, raw, normed_one, proj_a, proj_b, cosine, sine, starts,
+            query_scale[None], key_scale[None], mixed_own, grad_after_low, out_other, length,
         )
         attn_rows = scatter_z(attn_sum)
         attn_gain_grad = jnp.sum(grad_normed_one * inputs * inverse_rms(inputs), axis=0)

time: 644 us -> 646 us (level)
  no operation moved by 1% of the time
where the time goes in v1:
time: 646 us; the launch traced here: 638 us
  Pallas kernels  594 us (92%)
  local copies, waits for them, and re-layouts  19.3 us (3%)
  between operations  14.8 us (2%)
  other arithmetic  9.67 us (1%)
    pallas_call x1, Pallas kernels, attend_forward(): pl.pallas_call(attend_kernel, grid=(TP,), in_specs=[in_order(width)] + [i...  122 us
    pallas_call x1, Pallas kernels, attend_backward(): pl.pallas_call(attend_back_kernel, grid=(TP,), in_specs=[pl.BlockSpec(hea...  102 us
    pallas_call x1, Pallas kernels, down_forward(): pl.pallas_call(functools.partial(down_kernel, run), in_specs=[anywhere] *...  85.2 us
    pallas_call x1, Pallas kernels, feed_backward(): pl.pallas_call(feed_back_kernel, in_specs=[anywhere] * 7, out_specs=[pl.B...  83.5 us
    pallas_call x1, Pallas kernels, gather_group(): pl.pallas_call(functools.partial(gather_kernel, run), in_specs=[vmem] * 2...  73.5 us
    pallas_call x1, Pallas kernels, feed_forward(): pl.pallas_call(feed_kernel, in_specs=[anywhere] * 3, out_specs=[anywhere]...  63.6 us
    pallas_call x1, Pallas kernels, between(): pl.pallas_call(between_kernel, in_specs=[vmem] * 6 + [anywhere], out_spec...  32.7 us
    pallas_call x1, Pallas kernels, return_attention(): pl.pallas_call(return_kernel, in_specs=[pl.BlockSpec(memory_space=pl.ANY)...  15.7 us
  transfers between devices with their start and end apart: 6, of which 0 were waited for; matrix products, arithmetic and copies ran while one was open for 2% of the time, Pallas kernels for 88%

profile of v1, /device:TPU:1, one launch (start us, length us, event | category | flops | bytes accessed | tf_op | source)
XLA Modules:
  0.0 638.4 jit_solution(4405984849727671484)
XLA Ops:
  7.2 0.0 all-gather.6.cloned.1.call-start
  7.2 1.3 fusion.12
  8.6 14.8 %spread_attention.1 = (bf16[512,768]{1,0:T(8,128)(2,1)}, f32[8,1,256]{2,1,0:T(1,128)}, s32[4,1,384]{2,1,0:T(1,128)}) custom-call(bf16[64,2048]{1,0:T(8,128)(2,1)} %wq_ref.1, bf16[64,1024]{1,0:T(8,128)(2,1)} %wk_ref.1, bf16[64,1024]{1,0:T(8,128)(2,1)} %wv_ref.1, bf16[64,2048]{1,0:T(8,128)(2,1)} %wo_ref.1, f32[1,256]{1,0:T(1,128)} %bitcast.20, s32[1,384]{1,0:T(1,128)} %seg_ref.1), custom_call_target="tpu_custom_call" | custom-call | tf_op jit(solution)/shard_map/spread_attention/pallas_call | solution.py:789
  23.3 0.7 convert_element_type.63
  24.1 2.1 fusion.4
  26.1 0.0 all-gather.6.cloned.1.call-update
  26.2 0.0 all-gather.4.cloned.1.call-start
  26.2 0.1 maximum_bitcast_fusion
  26.3 0.6 pad_maximum_fusion.rate_ref
  26.9 73.5 %gather_group.1 = (f32[1536,128]{1,0:T(8,128)}, f32[1536,128]{1,0:T(8,128)}, s32[1536,1]{1,0:T(8,128)}, bf16[1536,2048]{1,0:T(8,128)(2,1)}, bf16[512,1536]{1,0:T(8,128)(2,1)}) custom-call(s32[4,1,384]{2,1,0:T(1,128)} %get-tuple-element.69.seg_ref, f32[2,128]{1,0:T(2,128)} %pad_maximum_fusion.rate_ref, bf16[384,2048]{1,0:T(8,128)(2,1)} %x_ref.2, ...), custom_call_target="tpu_custom_call" | custom-call | tf_op jit(solution)/shard_map/gather_group/pallas_call | solution.py:885
  100.4 0.0 all-gather.4.cloned.1.call-update
  100.5 0.0 all-gather.8.cloned.1.call-start
  100.5 0.0 all-gather.6.cloned.1.call-done
  100.5 0.7 slice_bitcast_fusion
  101.3 0.1 slice_convert_fusion.2
  101.3 0.7 reshape.129.ag_ref
  102.0 0.7 reshape.130.mg_ref.gain_ref
  102.7 0.1 slice_convert_fusion
  102.8 0.6 reshape.131.qg_ref
  103.4 0.6 reshape.132.kg_ref
  104.0 122.1 %attend_forward.1 = (f32[1536,1024]{1,0:T(8,128)}, bf16[1536,2048]{1,0:T(8,128)(2,1)}, bf16[384,2048]{1,0:T(8,128)(2,1)}, f32[384,2048]{1,0:T(8,128)}, f32[384,1...) custom-call(bf16[1536,2048]{1,0:T(8,128)(2,1)} %get-tuple-element.75, ...), custom_call_target="tpu_custom_call" | custom-call | flops 6442450944 | bytes 31457280 | tf_op jit(solution)/shard_map/attend_forward/pallas_call | solution.py:1091
  226.1 0.0 all-gather.4.cloned.1.call-done.wa_ref
  226.1 0.0 all-gather.8.cloned.1.call-update
  226.1 0.5 reduce-scatter.4.cloned.1.call-start
  226.6 63.6 %feed_forward.1 = (bf16[1536,1536]{1,0:T(8,128)(2,1)}, bf16[1536,1536]{1,0:T(8,128)(2,1)}, bf16[1536,1536]{1,0:T(8,128)(2,1)}, bf16[2048,1536]{1,0:T(8,128)(2,1)...) custom-call(bf16[1536,2048]{1,0:T(8,128)(2,1)} %get-tuple-element.81.a2_ref, ...), custom_call_target="tpu_custom_call" | custom-call | flops 9663676416 | bytes 31457280 | tf_op jit(solution)/shard_map/feed_forward/pallas_call | solution.py:483
  290.3 0.0 reduce-scatter.4.cloned.1.call-update
  290.3 0.0 reduce-scatter.8.cloned.1.call-start
  290.4 0.0 all-gather.8.cloned.1.call-done.da_ref
  290.4 83.5 %feed_backward.1 = (f32[384,2048]{1,0:T(8,128)}, bf16[2048,1536]{1,0:T(8,128)(2,1)}, bf16[768,2048]{1,0:T(8,128)(2,1)}, bf16[2048,1536]{1,0:T(8,128)(2,1)}) custom-call(bf16[1536,1536]{1,0:T(8,128)(2,1)} %get-tuple-element.83.gate_ref, bf16[1536,1536]{1,0:T(8,128)(2,1)} %get-tuple-element.84.up_ref, bf16[1536,2048]{1,0:T(8,128)(2,1)} %get-tuple-element.85.ga_ref, ...), custom_call_target="tpu_custom_call" | custom-call | flops 19327352832 | bytes 31457280 | tf_op jit(solution)/shard_map/feed_backward/pallas_call | solution.py:674
  373.8 0.0 reduce-scatter.8.cloned.1.call-update
  373.9 0.0 reduce-scatter.6.cloned.1.call-start
  373.9 0.0 reduce-scatter.4.cloned.1.call-done.down_ref
  373.9 32.7 %between.1 = (f32[384,2048]{1,0:T(8,128)}, bf16[384,2048]{1,0:T(8,128)(2,1)}, f32[1,2048]{1,0:T(1,128)}, bf16[4,384,512]{2,1,0:T(8,128)(2,1)}, bf16[4,2048,256]{2,1,0:T(8,128)(2,1)}) custom-call(f32[384,2048]{1,0:T(8,128)} %get-tuple-element.90.grad_ref, f32[384,2048]{1,0:T(8,128)} %get-tuple-element.91.after_ref, f32[384,1]{1,0:T(8,128)} %get-tuple-element.92.inv_ref, ...), custom_call_target="tpu_custom_call" | custom-call | flops 6442450944 | bytes 25165824 | tf_op jit(solution)/shard_map/between/pallas_call | solution.py:1221
  406.7 102.5 %attend_backward.1 = (f32[384,2048]{1,0:T(8,128)}, bf16[2048,768]{1,0:T(8,128)(2,1)}, f32[1,128]{1,0:T(1,128)}, f32[1,128]{1,0:T(1,128)}, bf16[3,2048,256]{2,1,0:T(8,128)(2,1)}) custom-call(bf16[4,384,512]{2,1,0:T(8,128)(2,1)} %get-tuple-element.95.heads, f32[1536,1024]{1,0:T(8,128)} %get-tuple-element.96.raw_ref, ...), custom_call_target="tpu_custom_call" | custom-call | flops 6442450944 | bytes 31457280 | tf_op jit(solution)/shard_map/attend_backward/pallas_call | solution.py:1260
  509.2 0.0 copy-start
  509.2 0.0 reduce-scatter.6.cloned.1.call-update
  509.2 1.4 copy-done
  510.6 0.4 fusion.2
  511.0 2.3 fusion.1
  513.4 0.1 reshape.124
  513.4 0.5 broadcast.61
  514.0 0.0 copy-done.11
  514.0 0.7 reduce.10
  514.6 0.1 reshape.126
  514.8 0.7 reduce.11
  515.4 0.1 reshape.127
  515.5 0.0 copy-done.9
  515.5 0.7 reduce.9
  516.2 0.1 reshape.125
  516.3 0.7 concatenate.15
  517.0 85.2 %down_forward.1 = (bf16[384,2048]{1,0:T(8,128)(2,1)}, f32[64,6144]{1,0:T(8,128)}, f32[64,6144]{1,0:T(8,128)}, f32[4,1,256]{2,1,0:T(1,128)}, bf16[384,2048]{1,0:T(8,128)(2,1)}, /*index=5*/f32[192,2048]{1,0:T(8,128)}) custom-call(bf16[1536,1536]{1,0:T(8,128)(2,1)} %get-tuple-element.103.hid_ref, bf16[768,2048]{1,0:T(8,128)(2,1)} %all-gather.8.cloned.1.call-done.da_ref, ...), custom_call_target="tpu_custom_call" | custom-call | flops 2415919104 | bytes 31457280 | tf_op jit(solution)/shard_map/down_forward/pallas_call | solution.py:1406
  602.3 0.0 reduce-scatter.6.cloned.1.call-done.rows_ref
  602.3 15.7 %return_attention.1 = (f32[64,2048]{1,0:T(8,128)}, f32[64,1024]{1,0:T(8,128)}, f32[64,1024]{1,0:T(8,128)}, f32[64,2048]{1,0:T(8,128)}, f32[1,256]{1,0:T(1,128)}) custom-call(bf16[512,768]{1,0:T(8,128)(2,1)} %reduce-scatter.6.cloned.1.call-done.rows_ref, f32[4,1,256]{2,1,0:T(1,128)} %get-tuple-element.116.gains_ref), custom_call_target="tpu_custom_call" | custom-call | tf_op jit(solution)/shard_map/return_attention/pallas_call | solution.py:1488
  618.0 1.3 slice_bitcast_fusion.3
  619.4 1.3 slice_bitcast_fusion.1
  620.7 2.8 copy.45
  623.5 1.1 copy.46
  624.6 0.8 copy.47
  625.4 0.7 copy.48
  626.1 0.7 copy.49
  626.8 0.8 copy.50
  627.6 1.1 copy.51
  628.8 1.1 copy.52
  629.9 1.1 copy.53
  (30 shorter events, 0.1 us)
Async XLA Ops:
  7.2 93.3 %all-gather.6.cloned.1.call-start = ((), (), s32[]{:S(2)}) async-start(), calls=%async_computation.4 | async-start | bytes 4055040 | tf_op jit(solution)/shard_map/all_gather | solution.py:1528
  26.2 199.9 %all-gather.4.cloned.1.call-start = ((), (), s32[]{:S(2)}) async-start(), calls=%async_computation.3 | async-start | bytes 7864320 | tf_op jit(solution)/shard_map/all_gather | solution.py:1528
  100.5 189.9 %all-gather.8.cloned.1.call-start = ((), (), s32[]{:S(2)}) async-start(), calls=%async_computation.5 | async-start | bytes 3932160 | tf_op jit(solution)/shard_map/all_gather | solution.py:1528
  226.1 147.8 %reduce-scatter.4.cloned.1.call-start = ((), (), s32[]{:S(2)}) async-start(), calls=%async_computation.6 | async-start | bytes 3932160 | tf_op jit(solution)/shard_map/reduce_scatter | solution.py:1531
  290.3 226.7 %reduce-scatter.8.cloned.1.call-start = ((), (), s32[]{:S(2)}) async-start(), calls=%async_computation.8 | async-start | bytes 7864320 | tf_op jit(solution)/shard_map/reduce_scatter | solution.py:1531
  373.9 228.5 %reduce-scatter.6.cloned.1.call-start = ((), (), s32[]{:S(2)}) async-start(), calls=%async_computation.7 | async-start | bytes 3932160 | tf_op jit(solution)/shard_map/reduce_scatter | solution.py:1531
  509.2 1.4 copy-start
  510.6 3.3 copy-start.11
  510.6 4.1 copy-start.10
  510.6 4.9 copy-start.9
  602.3 21.2 %copy-start.4 = (bf16[384,2048]{1,0:T(8,128)(2,1)S(1)}, bf16[384,2048]{1,0:T(8,128)(2,1)}, u32[]{:S(2)}) copy-start(bf16[384,2048]{1,0:T(8,128)(2,1)} %get-tuple-element.147) | copy-start | bytes 4718596
  620.7 4.0 copy-start.6
  620.7 4.8 copy-start.8
  623.5 2.7 copy-start.7
  623.5 3.4 copy-start.5
  623.5 4.2 copy-start.3
  624.6 4.2 copy-start.2
  627.6 2.3 copy-start.1
Sparse Core Ops, SparseCore 0:
  26.3 65.9 all-gather.5
  100.6 115.9 all-gather.3
  226.2 63.1 all-gather.7
  291.6 58.7 reduce-scatter.3
  374.0 113.4 reduce-scatter.7
  509.4 62.2 reduce-scatter.5

commit v2 on v1

--- a/solution.py
+++ b/solution.py
@@ -173,7 +173,7 @@
 def attend_back_kernel(
     heads, raw_ref, a1_ref, pa_ref, pb_ref, cos_ref, sin_ref, start_ref, qg_ref, kg_ref, mix_ref, dy_ref, orecv_ref,
     out_ref, sum_ref, dqg_ref, dkg_ref, ogot_ref,
-    gp_ref, dk_ref, dv_ref, acc_a, acc_b, cbuf, crecv, oslot, ofetch,
+    gp_ref, dk_ref, dv_ref, acc_a, acc_b, cbuf, crecv, oslot, ofetch, dyo,
     ebuf, rd, rxy, rs_send, rs_recv, c_send, c_recv, os_send, os_recv, o_local,
 ):
     length = a1_ref.shape[0]
@@ -201,39 +201,36 @@
         pltpu.make_async_copy(ogot_ref.at[k - 1], oslot.at[k], o_local.at[k]) for k in range(1, 3)
     ]
 
-    def out_block(k, side):
-        device = (me, x, y, d)[k]
-        at = ((device // 2) % TP) * 2 + side
-        return pl.ds(pl.multiple_of(at * block, block), block)
-
-    def out_tile(k, side, sl):
-        return dot_tn(mix_ref[:, sl], dy_ref[:, out_block(k, side)])
-
     @pl.when(s == 0)
     def _():
+        fetch = pltpu.make_async_copy(orecv_ref, oslot, o_local.at[0])
+        fetch.start()
         greet((x, y, d, sibling))
         for ref in (acc_a, acc_b, dqg_ref, dkg_ref):
             ref[...] = jnp.zeros_like(ref)
-        for k in (3, 1, 2, 0):
-            fetch = pltpu.make_async_copy(orecv_ref.at[k], ofetch, o_local.at[0])
-            fetch.start()
-            fetch.wait()
-
-            @pl.loop(0, oslot.shape[1] // TILE)
-            def _(t):
-                sl = pl.ds(pl.multiple_of(t * TILE, TILE), TILE)
-                oslot[k, sl, :] = (out_tile(k, core, sl) + ofetch[sl, :].astype(f32)).astype(bf16)
-
-            if k == 3:
-                o_low.start()
-                o_high.start()
+        for k, device in enumerate((me, x, y, d)):
+            at = ((device // 2) % TP) * 2 + core
+            dyo[:, k * block : (k + 1) * block] = dy_ref[:, pl.ds(pl.multiple_of(at * block, block), block)]
+        fetch.wait()
+
+        @pl.loop(0, oslot.shape[1] // TILE)
+        def _(t):
+            sl = pl.ds(pl.multiple_of(t * TILE, TILE), TILE)
+            value = dot_tn(mix_ref[:, sl], dyo[...])
+            for k in range(TP):
+                oslot[k, sl, :] = (
+                    value[:, k * block : (k + 1) * block] + oslot[k, sl, :].astype(f32)
+                ).astype(bf16)
+
+        o_low.start()
+        o_high.start()
 
     @pl.when(s == 1)
     def _():
         for copy, k, offset in ((o_low, 1, 0), (o_high, 2, tall)):
             copy.wait_recv()
             fetch = pltpu.make_async_copy(
-                ogot_ref.at[2, pl.ds(offset, tall)], ofetch.at[pl.ds(0, tall)], o_local.at[0]
+                ogot_ref.at[2, pl.ds(offset, tall)], ofetch, o_local.at[0]
             )
             fetch.start()
             fetch.wait()
@@ -1143,7 +1140,7 @@
 def between_kernel(
     grad_ref, after_ref, inv_ref, gain_ref, cot_ref, mix_ref, w_ref,
     sum_ref, dy_ref, dgain_ref, heads_ref, orecv_ref,
-    w, heads, oslot, loads, h_send, h_recv, o_send, o_recv,
+    w, heads, oslot, dyo, loads, h_send, h_recv, o_send, o_recv,
 ):
     length, width = after_ref.shape
     step = 128
@@ -1166,9 +1163,10 @@
         for k in range(1, TP)
     ]
     keep = pltpu.make_async_copy(heads.at[0], heads_ref.at[0], loads.at[TP])
-    across = [
-        remote(oslot.at[k], orecv_ref.at[k], o_send.at[k], o_recv.at[k], sibling) for k in range(TP)
-    ]
+    def across(t):
+        sl = pl.ds(pl.multiple_of(t * TILE, TILE), TILE)
+        return remote(oslot.at[:, sl], orecv_ref.at[:, sl], o_send.at[t], o_recv.at[t], sibling)
+
     for k in ORDER:
         load[k].start()
     greet((x, y, d, sibling))
@@ -1185,18 +1183,6 @@
         dy_ref[sl, :] = total.astype(bf16)
         dgain_ref[...] += jnp.sum(grad * values * inverse, axis=0, keepdims=True)
 
-    def out_half(k):
-        at = ((places[k] // 2) % TP) * 2 + 1 - core
-        cut = pl.ds(pl.multiple_of(at * block, block), block)
-
-        @pl.loop(0, oslot.shape[1] // TILE)
-        def _(t):
-            sl = pl.ds(pl.multiple_of(t * TILE, TILE), TILE)
-            oslot[k, sl, :] = dot_tn(mix_ref[:, sl], dy_ref[:, cut]).astype(bf16)
-
-        across[k].start()
-
-    out_half(3)
     for k in ORDER:
         load[k].wait()
         heads[k] = dot_nt(dy_ref[...], w[k]).astype(bf16)
@@ -1204,10 +1190,24 @@
             home[k - 1].start()
         else:
             keep.start()
-    for k in ORDER[1:]:
-        out_half(k)
-    for copy in home + across:
+    for k in range(TP):
+        at = ((places[k] // 2) % TP) * 2 + 1 - core
+        dyo[:, k * block : (k + 1) * block] = dy_ref[:, pl.ds(pl.multiple_of(at * block, block), block)]
+
+    tiles = oslot.shape[1] // TILE
+
+    @pl.loop(0, tiles)
+    def _(t):
+        sl = pl.ds(pl.multiple_of(t * TILE, TILE), TILE)
+        value = dot_tn(mix_ref[:, sl], dyo[...])
+        for k in range(TP):
+            oslot[k, sl, :] = value[:, k * block : (k + 1) * block].astype(bf16)
+        across(t).start()
+
+    for copy in home:
         copy.wait()
+    for t in range(tiles):
+        across(t).wait()
     keep.wait()
 
 
@@ -1233,7 +1233,8 @@
             pltpu.VMEM((TP, cols, width), bf16),
             pltpu.VMEM((TP, length, cols), bf16),
             pltpu.VMEM((TP, width, block), bf16),
-            sem((TP + 1,)), sem((3,)), sem((3,)), sem((TP,)), sem((TP,)),
+            pltpu.VMEM((length, TP * block), bf16),
+            sem((TP + 1,)), sem((3,)), sem((3,)), sem((width // TILE,)), sem((width // TILE,)),
         ],
         compiler_params=pltpu.CompilerParams(
             vmem_limit_bytes=60 << 20, collective_id=9, has_side_effects=True
@@ -1282,7 +1283,8 @@
             pltpu.VMEM(pa.shape, bf16),
             pltpu.VMEM(pa.shape, bf16),
             pltpu.VMEM((TP, width, block), bf16),
-            pltpu.VMEM((width, block), bf16),
+            pltpu.VMEM((width // 2, block), bf16),
+            pltpu.VMEM((length, TP * block), bf16),
         ]
         + scatter_scratch(length, width)
         + [sem, sem, sem((4,)), sem((4,)), sem((TP,))],

time: 646 us -> 643 us (level)
  no operation moved by 1% of the time
where the time goes in v2:
time: 643 us; the launch traced here: 635 us
  Pallas kernels  591 us (92%)
  local copies, waits for them, and re-layouts  19.3 us (3%)
  between operations  14.6 us (2%)
  other arithmetic  9.67 us (2%)
    pallas_call x1, Pallas kernels, attend_forward(): pl.pallas_call(attend_kernel, grid=(TP,), in_specs=[in_order(width)] + [i...  122 us
    pallas_call x1, Pallas kernels, attend_backward(): pl.pallas_call(attend_back_kernel, grid=(TP,), in_specs=[pl.BlockSpec(hea...  100 us
    pallas_call x1, Pallas kernels, down_forward(): pl.pallas_call(functools.partial(down_kernel, run), in_specs=[anywhere] *...  85.1 us
    pallas_call x1, Pallas kernels, feed_backward(): pl.pallas_call(feed_back_kernel, in_specs=[anywhere] * 7, out_specs=[pl.B...  83.9 us
    pallas_call x1, Pallas kernels, gather_group(): pl.pallas_call(functools.partial(gather_kernel, run), in_specs=[vmem] * 2...  73.5 us
    pallas_call x1, Pallas kernels, feed_forward(): pl.pallas_call(feed_kernel, in_specs=[anywhere] * 3, out_specs=[anywhere]...  63.6 us
    pallas_call x1, Pallas kernels, between(): pl.pallas_call(between_kernel, in_specs=[vmem] * 6 + [anywhere], out_spec...  31.8 us
    pallas_call x1, Pallas kernels, return_attention(): pl.pallas_call(return_kernel, in_specs=[pl.BlockSpec(memory_space=pl.ANY)...  15.9 us
  transfers between devices with their start and end apart: 6, of which 0 were waited for; matrix products, arithmetic and copies ran while one was open for 2% of the time, Pallas kernels for 88%

profile of v2, /device:TPU:1, one launch (start us, length us, event | category | flops | bytes accessed | tf_op | source)
XLA Modules:
  0.0 635.1 jit_solution(4365292839679566976)
XLA Ops:
  7.2 0.0 all-gather.6.cloned.1.call-start
  7.2 1.3 fusion.12
  8.6 14.8 %spread_attention.1 = (bf16[512,768]{1,0:T(8,128)(2,1)}, f32[8,1,256]{2,1,0:T(1,128)}, s32[4,1,384]{2,1,0:T(1,128)}) custom-call(bf16[64,2048]{1,0:T(8,128)(2,1)} %wq_ref.1, bf16[64,1024]{1,0:T(8,128)(2,1)} %wk_ref.1, bf16[64,1024]{1,0:T(8,128)(2,1)} %wv_ref.1, bf16[64,2048]{1,0:T(8,128)(2,1)} %wo_ref.1, f32[1,256]{1,0:T(1,128)} %bitcast.20, s32[1,384]{1,0:T(1,128)} %seg_ref.1), custom_call_target="tpu_custom_call" | custom-call | tf_op jit(solution)/shard_map/spread_attention/pallas_call | solution.py:786
  23.3 0.7 convert_element_type.63
  24.1 2.1 fusion.4
  26.1 0.0 all-gather.6.cloned.1.call-update
  26.2 0.0 all-gather.4.cloned.1.call-start
  26.2 0.1 maximum_bitcast_fusion
  26.3 0.6 pad_maximum_fusion.rate_ref
  26.9 73.5 %gather_group.1 = (f32[1536,128]{1,0:T(8,128)}, f32[1536,128]{1,0:T(8,128)}, s32[1536,1]{1,0:T(8,128)}, bf16[1536,2048]{1,0:T(8,128)(2,1)}, bf16[512,1536]{1,0:T(8,128)(2,1)}) custom-call(s32[4,1,384]{2,1,0:T(1,128)} %get-tuple-element.69.seg_ref, f32[2,128]{1,0:T(2,128)} %pad_maximum_fusion.rate_ref, bf16[384,2048]{1,0:T(8,128)(2,1)} %x_ref.2, ...), custom_call_target="tpu_custom_call" | custom-call | tf_op jit(solution)/shard_map/gather_group/pallas_call | solution.py:882
  100.4 0.0 all-gather.4.cloned.1.call-update
  100.5 0.0 all-gather.8.cloned.1.call-start
  100.5 0.0 all-gather.6.cloned.1.call-done
  100.5 0.7 slice_bitcast_fusion
  101.3 0.1 slice_convert_fusion.2
  101.3 0.7 reshape.129.ag_ref
  102.0 0.7 reshape.130.mg_ref.gain_ref
  102.7 0.1 slice_convert_fusion
  102.8 0.6 reshape.131.qg_ref
  103.4 0.6 reshape.132.kg_ref
  104.0 122.1 %attend_forward.1 = (f32[1536,1024]{1,0:T(8,128)}, bf16[1536,2048]{1,0:T(8,128)(2,1)}, bf16[384,2048]{1,0:T(8,128)(2,1)}, f32[384,2048]{1,0:T(8,128)}, f32[384,1...) custom-call(bf16[1536,2048]{1,0:T(8,128)(2,1)} %get-tuple-element.75, ...), custom_call_target="tpu_custom_call" | custom-call | flops 6442450944 | bytes 31457280 | tf_op jit(solution)/shard_map/attend_forward/pallas_call | solution.py:1088
  226.1 0.0 all-gather.4.cloned.1.call-done.wa_ref
  226.1 0.0 all-gather.8.cloned.1.call-update
  226.1 0.3 reduce-scatter.4.cloned.1.call-start
  226.4 63.6 %feed_forward.1 = (bf16[1536,1536]{1,0:T(8,128)(2,1)}, bf16[1536,1536]{1,0:T(8,128)(2,1)}, bf16[1536,1536]{1,0:T(8,128)(2,1)}, bf16[2048,1536]{1,0:T(8,128)(2,1)...) custom-call(bf16[1536,2048]{1,0:T(8,128)(2,1)} %get-tuple-element.81.a2_ref, ...), custom_call_target="tpu_custom_call" | custom-call | flops 9663676416 | bytes 31457280 | tf_op jit(solution)/shard_map/feed_forward/pallas_call | solution.py:480
  290.0 0.0 reduce-scatter.4.cloned.1.call-update
  290.0 0.0 reduce-scatter.8.cloned.1.call-start
  290.1 0.0 all-gather.8.cloned.1.call-done.da_ref
  290.1 83.9 %feed_backward.1 = (f32[384,2048]{1,0:T(8,128)}, bf16[2048,1536]{1,0:T(8,128)(2,1)}, bf16[768,2048]{1,0:T(8,128)(2,1)}, bf16[2048,1536]{1,0:T(8,128)(2,1)}) custom-call(bf16[1536,1536]{1,0:T(8,128)(2,1)} %get-tuple-element.83.gate_ref, bf16[1536,1536]{1,0:T(8,128)(2,1)} %get-tuple-element.84.up_ref, bf16[1536,2048]{1,0:T(8,128)(2,1)} %get-tuple-element.85.ga_ref, ...), custom_call_target="tpu_custom_call" | custom-call | flops 19327352832 | bytes 31457280 | tf_op jit(solution)/shard_map/feed_backward/pallas_call | solution.py:671
  374.0 0.0 reduce-scatter.8.cloned.1.call-update
  374.0 0.0 reduce-scatter.6.cloned.1.call-start
  374.1 0.0 reduce-scatter.4.cloned.1.call-done.down_ref
  374.1 31.8 %between.1 = (f32[384,2048]{1,0:T(8,128)}, bf16[384,2048]{1,0:T(8,128)(2,1)}, f32[1,2048]{1,0:T(1,128)}, bf16[4,384,512]{2,1,0:T(8,128)(2,1)}, bf16[4,2048,256]{2,1,0:T(8,128)(2,1)}) custom-call(f32[384,2048]{1,0:T(8,128)} %get-tuple-element.90.grad_ref, f32[384,2048]{1,0:T(8,128)} %get-tuple-element.91.after_ref, f32[384,1]{1,0:T(8,128)} %get-tuple-element.92.inv_ref, ...), custom_call_target="tpu_custom_call" | custom-call | flops 6442450944 | bytes 25165824 | tf_op jit(solution)/shard_map/between/pallas_call | solution.py:1221
  405.9 100.2 %attend_backward.1 = (f32[384,2048]{1,0:T(8,128)}, bf16[2048,768]{1,0:T(8,128)(2,1)}, f32[1,128]{1,0:T(1,128)}, f32[1,128]{1,0:T(1,128)}, bf16[3,2048,256]{2,1,0:T(8,128)(2,1)}) custom-call(bf16[4,384,512]{2,1,0:T(8,128)(2,1)} %get-tuple-element.95.heads, f32[1536,1024]{1,0:T(8,128)} %get-tuple-element.96.raw_ref, ...), custom_call_target="tpu_custom_call" | custom-call | flops 6442450944 | bytes 31457280 | tf_op jit(solution)/shard_map/attend_backward/pallas_call | solution.py:1261
  506.1 0.0 copy-start
  506.1 0.0 reduce-scatter.6.cloned.1.call-update
  506.1 1.4 copy-done
  507.5 0.4 fusion.2
  507.9 2.3 fusion.1
  510.3 0.1 reshape.124
  510.3 0.5 broadcast.61
  510.9 0.7 reduce.10
  511.5 0.1 reshape.126
  511.7 0.7 reduce.11
  512.3 0.1 reshape.127
  512.5 0.7 reduce.9
  513.1 0.1 reshape.125
  513.2 0.7 concatenate.15
  514.0 85.1 %down_forward.1 = (bf16[384,2048]{1,0:T(8,128)(2,1)}, f32[64,6144]{1,0:T(8,128)}, f32[64,6144]{1,0:T(8,128)}, f32[4,1,256]{2,1,0:T(1,128)}, bf16[384,2048]{1,0:T(8,128)(2,1)}, /*index=5*/f32[192,2048]{1,0:T(8,128)}) custom-call(bf16[1536,1536]{1,0:T(8,128)(2,1)} %get-tuple-element.103.hid_ref, bf16[768,2048]{1,0:T(8,128)(2,1)} %all-gather.8.cloned.1.call-done.da_ref, ...), custom_call_target="tpu_custom_call" | custom-call | flops 2415919104 | bytes 31457280 | tf_op jit(solution)/shard_map/down_forward/pallas_call | solution.py:1408
  599.0 0.0 copy-start.4
  599.1 0.0 reduce-scatter.6.cloned.1.call-done.rows_ref
  599.1 15.9 %return_attention.1 = (f32[64,2048]{1,0:T(8,128)}, f32[64,1024]{1,0:T(8,128)}, f32[64,1024]{1,0:T(8,128)}, f32[64,2048]{1,0:T(8,128)}, f32[1,256]{1,0:T(1,128)}) custom-call(bf16[512,768]{1,0:T(8,128)(2,1)} %reduce-scatter.6.cloned.1.call-done.rows_ref, f32[4,1,256]{2,1,0:T(1,128)} %get-tuple-element.116.gains_ref), custom_call_target="tpu_custom_call" | custom-call | tf_op jit(solution)/shard_map/return_attention/pallas_call | solution.py:1490
  615.0 1.3 slice_bitcast_fusion.3
  616.3 1.3 slice_bitcast_fusion.1
  617.6 2.8 copy.45
  620.4 1.1 copy.46
  621.6 0.0 copy-done.6
  621.6 0.8 copy.47
  622.4 0.7 copy.48
  623.1 0.7 copy.49
  623.8 0.8 copy.50
  624.6 1.1 copy.51
  625.7 1.1 copy.52
  626.9 1.1 copy.53
  (30 shorter events, 0.1 us)
Async XLA Ops:
  7.2 93.3 %all-gather.6.cloned.1.call-start = ((), (), s32[]{:S(2)}) async-start(), calls=%async_computation.4 | async-start | bytes 4055040 | tf_op jit(solution)/shard_map/all_gather | solution.py:1530
  26.2 199.9 %all-gather.4.cloned.1.call-start = ((), (), s32[]{:S(2)}) async-start(), calls=%async_computation.3 | async-start | bytes 7864320 | tf_op jit(solution)/shard_map/all_gather | solution.py:1530
  100.5 189.7 %all-gather.8.cloned.1.call-start = ((), (), s32[]{:S(2)}) async-start(), calls=%async_computation.5 | async-start | bytes 3932160 | tf_op jit(solution)/shard_map/all_gather | solution.py:1530
  226.1 148.0 %reduce-scatter.4.cloned.1.call-start = ((), (), s32[]{:S(2)}) async-start(), calls=%async_computation.6 | async-start | bytes 3932160 | tf_op jit(solution)/shard_map/reduce_scatter | solution.py:1533
  290.0 223.9 %reduce-scatter.8.cloned.1.call-start = ((), (), s32[]{:S(2)}) async-start(), calls=%async_computation.8 | async-start | bytes 7864320 | tf_op jit(solution)/shard_map/reduce_scatter | solution.py:1533
  374.0 225.1 %reduce-scatter.6.cloned.1.call-start = ((), (), s32[]{:S(2)}) async-start(), calls=%async_computation.7 | async-start | bytes 3932160 | tf_op jit(solution)/shard_map/reduce_scatter | solution.py:1533
  506.1 1.4 copy-start
  507.5 3.3 copy-start.11
  507.5 4.1 copy-start.10
  507.5 4.9 copy-start.9
  599.0 21.4 %copy-start.4 = (bf16[384,2048]{1,0:T(8,128)(2,1)S(1)}, bf16[384,2048]{1,0:T(8,128)(2,1)}, u32[]{:S(2)}) copy-start(bf16[384,2048]{1,0:T(8,128)(2,1)} %get-tuple-element.147) | copy-start | bytes 4718596
  617.6 4.0 copy-start.6
  617.6 4.8 copy-start.8
  620.4 2.7 copy-start.7
  620.4 3.4 copy-start.5
  620.4 4.2 copy-start.3
  621.6 4.2 copy-start.2
  624.6 2.3 copy-start.1
Sparse Core Ops, SparseCore 0:
  26.3 65.9 all-gather.5
  100.6 115.9 all-gather.3
  226.2 63.2 all-gather.7
  291.7 58.7 reduce-scatter.3
  374.1 112.8 reduce-scatter.7
  506.3 61.4 reduce-scatter.5
